TPU v7x, 1024 devices: a whole 4x4x32 slice. The times are simulated.
1024 devices in a mesh: tensor: 16 (over x, y), dp: 64 (over z, core).
Axes of the slice: x: 4, y: 4, z: 32, core: 2. Of those that a mesh axis runs over, the one named last changes fastest.
Arguments:
- tokens: bfloat16 [1024, 8192], P('dp', 'tensor'), may hold values from -6 to 6
- pad_mask: int32 [1024], P('dp'), may hold values 0 or 1
- gate_weight: bfloat16 [8192, 28672], P('tensor', 'dp'), may hold values from -0.0625 to 0.0625
- up_weight: bfloat16 [8192, 28672], P('tensor', 'dp'), may hold values from -0.0625 to 0.0625
- down_weight: bfloat16 [28672, 8192], P('dp', 'tensor'), may hold values from -0.03125 to 0.03125
Outputs:
- mixed: bfloat16 [1024, 8192], P('dp', 'tensor')
All inputs are finite; a program needn't handle non-finite values. No bound on the sum of `pad_mask` on one device may be relied on, other than what follows from the above.
Results may differ from a plain program's by a relative error of at most 0.028.
Values may be sent and summed in bfloat16 or wider, within the bound.
No kernel may reach another device: no remote copies, remote signals or barrier semaphores. Data moves between devices by JAX's collectives and lax.ppermute only.
A program may use at most 32 MiB of HBM per device.

v0:
```python
import jax
import jax.numpy as jnp
from jax import lax
from jax.sharding import PartitionSpec as P


def activate(sums, width):
    gate = sums[:, :width]
    up = sums[:, width:]
    sigma = jax.nn.sigmoid(gate)
    return (gate * sigma * up).astype(jnp.bfloat16)


def on_device(tokens, pad_mask, gate_weight, up_weight, down_weight):
    width = gate_weight.shape[1]
    all_tokens = lax.all_gather(tokens, "dp", axis=0, tiled=True)
    paired = jnp.concatenate([gate_weight, up_weight], axis=1)
    summed = lax.psum_scatter(
        jnp.dot(all_tokens, paired, preferred_element_type=jnp.float32).astype(jnp.bfloat16),
        "tensor",
        scatter_dimension=0,
        tiled=True,
    ).astype(jnp.float32)
    hidden = lax.all_gather(activate(summed, width), "tensor", axis=0, tiled=True)
    result = lax.psum_scatter(
        jnp.dot(hidden, down_weight, preferred_element_type=jnp.float32),
        "dp",
        scatter_dimension=0,
        tiled=True,
    )
    return (result * pad_mask[:, None].astype(jnp.float32)).astype(jnp.bfloat16)


def solution(mesh):
    placed = (P("dp", "tensor"), P("dp"), P("tensor", "dp"), P("tensor", "dp"), P("dp", "tensor"))
    return jax.shard_map(
        on_device, mesh=mesh, in_specs=placed, out_specs=P("dp", "tensor"), check_vma=False
    )
```

profile of v0, /device:TPU:2, one launch (start us, length us, event | category | flops | bytes accessed | tf_op | source)
XLA Modules:
  0.0 504.9 jit_solution(12767408406538198455)
XLA Ops:
  6.5 0.0 copy-start
  6.5 0.0 all-gather.2.cloned.1.call-start
  6.5 0.7 all-gather.2.cloned.1.call-update
  7.3 0.0 reduce-scatter.7.cloned.1.call-start
  7.3 145.6 %all-gather.2.cloned.1.call-done = bf16[1024,512]{1,0:T(8,128)(2,1)} async-done(((bf16[16,512]{1,0:T(8,128)(2,1)}), bf16[1024,512]{1,0:T(8,128)(2,1)}) %all-gather.2.cloned.1.call-update) | async-done | bytes 1048592 | tf_op jit(solution)/shard_map/all_gather | solution.py:16
  152.9 2.7 convert_bitcast_fusion
  155.6 2.5 copy.8
  158.1 0.0 reduce-scatter.7.cloned.1.call-update
  158.1 0.0 reduce-scatter.5.cloned.1.call-start
  158.1 101.1 %reduce-scatter.7.cloned.1.call-done = bf16[64,896]{1,0:T(8,128)(2,1)} async-done(((bf16[1024,896]{1,0:T(8,128)(2,1)}), bf16[64,896]{1,0:T(8,128)(2,1)}) %reduce-scatter.7.cloned.1.call-update) | async-done | bytes 114704 | tf_op jit(solution)/shard_map/reduce_scatter | solution.py:18
  259.2 0.9 convert_element_type.21
  260.1 0.1 fusion.3
  260.2 23.1 %all_gather.7 = bf16[1024,448]{1,0:T(8,128)(2,1)S(1)} all-gather(bf16[64,448]{1,0:T(8,128)(2,1)S(1)} %fusion.3), channel_id=1, replica_groups=mesh['tensor'=16,'dp'=64] {'tensor'}, dimensions={0}, use_global_device_ids=true | all-gather | bytes 974848 | tf_op jit(solution)/shard_map/all_gather | solution.py:24
  283.3 0.0 copy-done
  283.3 2.0 fusion.5
  285.4 0.0 copy-start.1
  285.4 0.0 reduce-scatter.5.cloned.1.call-update
  285.4 0.6 copy-done.1
  286.0 210.9 %reduce-scatter.5.cloned.1.call-done = f32[16,512]{1,0:T(8,128)} async-done(((f32[1024,512]{1,0:T(8,128)}), f32[16,512]{1,0:T(8,128)}) %reduce-scatter.5.cloned.1.call-update) | async-done | bytes 32784 | tf_op jit(solution)/shard_map/reduce_scatter | solution.py:25
  496.9 1.4 multiply_convert_fusion
  (1 shorter events, 0.0 us)
Async XLA Ops:
  6.5 276.8 %copy-start = (bf16[448,512]{1,0:T(8,128)(2,1)S(1)}, bf16[448,512]{1,0:T(8,128)(2,1)}, u32[]{:S(2)}) copy-start(bf16[448,512]{1,0:T(8,128)(2,1)} %param.9) | copy-start | bytes 1376260
  6.5 146.4 %all-gather.2.cloned.1.call-start = ((), (), s32[]{:S(2)}) async-start(), calls=%async_computation.2 | async-start | bytes 1064960 | tf_op jit(solution)/shard_map/all_gather | solution.py:16
  7.3 252.0 %reduce-scatter.7.cloned.1.call-start = ((), (), s32[]{:S(2)}) async-start(), calls=%async_computation.4 | async-start | bytes 1949696 | tf_op jit(solution)/shard_map/reduce_scatter | solution.py:18
  158.1 338.8 %reduce-scatter.5.cloned.1.call-start = ((), (), s32[]{:S(2)}) async-start(), calls=%async_computation.3 | async-start | bytes 2129920 | tf_op jit(solution)/shard_map/reduce_scatter | solution.py:25
  285.4 0.7 copy-start.1
Sparse Core Ops, SparseCore 0:
  10.1 142.8 all-gather.1
  158.2 100.9 reduce-scatter.6
  285.5 211.3 reduce-scatter.4
where the time goes:
time: 505 us
  waiting for transfers between devices  458 us (91%)
  blocking collectives  23.1 us (5%)
  between operations  13.1 us (3%)
    reduce_scatter x1, waiting for transfers between devices, on_device(): lax.psum_scatter(jnp.dot(hidden, down_weight, preferred_element_type=jnp....  211 us
    all_gather x1, waiting for transfers between devices, on_device(): all_tokens = lax.all_gather(tokens, 'dp', axis=0, tiled=True)  146 us
    reduce_scatter x1, waiting for transfers between devices, on_device(): lax.psum_scatter(jnp.dot(all_tokens, paired, preferred_element_type=jnp.f...  101 us
    all_gather x1, blocking collectives, on_device(): lax.all_gather(activate(summed, width), 'tensor', axis=0, tiled=True)  23.1 us
  transfers between devices with their start and end apart: 3, of which 3 were waited for; matrix products, arithmetic and copies ran while one was open for 0% of the time, Pallas kernels for 0%

commit v1 on v0

v1 whole, which is shorter than its diff:
```python
import jax
import jax.numpy as jnp
from jax import lax
from jax.sharding import Mesh, PartitionSpec as P

X, Y, ZH, ZL, C = 4, 4, 8, 4, 2
DP = ("zh", "zl", "c")
TENSOR = ("x", "y")
F32 = jnp.float32
BF16 = jnp.bfloat16


def exchange(pieces, axes):
    return lax.all_to_all(pieces, axes, split_axis=0, concat_axis=0, tiled=True)


def spread(block, count, axes):
    return exchange(jnp.broadcast_to(block[None], (count,) + block.shape), axes)


def swap_cores(block):
    return lax.ppermute(block, "c", [(0, 1), (1, 0)])


def on_device(tokens, pad_mask, gate_weight, up_weight, down_weight):
    rows, feats = tokens.shape
    width = gate_weight.shape[1]
    sub = rows // X

    far = spread(tokens, ZH, "zh")
    far = far.reshape(ZH, X, sub, feats).transpose(1, 0, 2, 3).reshape(X, 1, ZH * sub, feats)
    far = jnp.broadcast_to(far, (X, ZL, ZH * sub, feats)).reshape(X * ZL, ZH * sub, feats)
    own = exchange(far, ("x", "zl")).reshape(X, ZL, 1, ZH * sub, feats)

    gates = spread(gate_weight, X, "x")
    ups = spread(up_weight, X, "x")
    downs = spread(down_weight, X, "x")

    lhs = jnp.concatenate([own, swap_cores(own)], axis=2)
    count = ZL * C * ZH * sub
    lhs = lhs.reshape(X, count, feats).transpose(1, 0, 2).reshape(count, X * feats)
    gate = jnp.dot(lhs, gates.reshape(X * feats, width), preferred_element_type=F32).astype(BF16)
    up = jnp.dot(lhs, ups.reshape(X * feats, width), preferred_element_type=F32).astype(BF16)
    sums = exchange(jnp.concatenate([gate, up], axis=1).reshape(Y, count // Y, 2 * width), "y")
    sums = jnp.sum(sums.astype(F32), axis=0)
    gate, up = sums[:, :width], sums[:, width:]
    hidden = (gate * jax.nn.sigmoid(gate) * up).astype(BF16)
    hidden = spread(hidden, Y, "y").reshape(count, width)

    part = jnp.einsum("tn,xnf->xtf", hidden, downs, preferred_element_type=F32)
    part = part.reshape(X, ZL, C, ZH * sub, feats)
    other = swap_cores(part[:, :, 1].astype(BF16))
    part = (part[:, :, 0] + other.astype(F32)).astype(BF16)
    part = exchange(part.reshape(X * ZL, ZH * sub, feats), ("x", "zl"))
    part = jnp.sum(part.reshape(X, ZL, ZH * sub, feats).astype(F32), axis=1).astype(BF16)
    part = part.reshape(X, ZH, sub, feats).transpose(1, 0, 2, 3).reshape(ZH, rows, feats)
    result = jnp.sum(exchange(part, "zh").astype(F32), axis=0)
    return (result * pad_mask[:, None].astype(F32)).astype(BF16)


def solution(mesh):
    fine = Mesh(mesh.devices.reshape(X, Y, ZH, ZL, C), TENSOR + DP)
    placed = (P(DP, TENSOR), P(DP), P(TENSOR, DP), P(TENSOR, DP), P(DP, TENSOR))
    return jax.shard_map(
        on_device, mesh=fine, in_specs=placed, out_specs=P(DP, TENSOR), check_vma=False
    )
```

time: 505 us -> 243 us (0.48)
  the two profiles are of different devices: /device:TPU:2 before, /device:TPU:8 now
where the time goes in v1:
time: 243 us; the launch traced here: 242 us
  blocking collectives  118 us (49%)
  waiting for transfers between devices  87.3 us (36%)
  starting transfers between devices  24.1 us (10%)
  local copies, waits for them, and re-layouts  7.39 us (3%)
  matrix products  4.22 us (2%)
    all_to_all x5, blocking collectives, exchange(): return lax.all_to_all(pieces, axes, split_axis=0, concat_axis=0, tiled=True)  118 us
    all_to_all x4, waiting for transfers between devices, exchange(): return lax.all_to_all(pieces, axes, split_axis=0, concat_axis=0, tiled=True)  83.6 us
    all_to_all x4, starting transfers between devices, exchange(): return lax.all_to_all(pieces, axes, split_axis=0, concat_axis=0, tiled=True)  20.3 us
    broadcast_in_dim x5, local copies, waits for them, and re-layouts, spread(): return exchange(jnp.broadcast_to(block[None], (count,) + block.shape), axes)  5.93 us
  transfers between devices with their start and end apart: 6, of which 6 were waited for; matrix products, arithmetic and copies ran while one was open for 1% of the time, Pallas kernels for 0%

profile of v1, /device:TPU:8, one launch (start us, length us, event | category | flops | bytes accessed | tf_op | source)
XLA Modules:
  0.0 242.2 jit_solution(13368320755047524802)
XLA Ops:
  0.0 0.7 broadcast_in_dim.14
  0.7 55.9 %all_to_all.45 = bf16[8,16,512]{2,1,0:T(8,128)(2,1)S(1)} all-to-all(bf16[8,16,512]{2,1,0:T(8,128)(2,1)S(1)} %broadcast_in_dim.14), channel_id=1, replica_groups=mesh['x'=4,'y'=4,'zh'=8,'zl'=4,'c'=2] {'zh'}, dimensions={0} | all-to-all | bytes 262144 | tf_op jit(solution)/shard_map/all_to_all | solution.py:14
  56.7 2.4 broadcast_in_dim.17
  59.1 4.3 %all-to-all-start.2 = ((bf16[4,512,448]{1,2,0:T(8,128)(2,1)}), bf16[4,512,448]{1,2,0:T(8,128)(2,1)S(1)}, u32[]{:S(2)}, u32[]{:S(2)}) async-start(bf16[4,512,448]{1,2,0:T(8,128)(2,1)} %broadcast_in_dim.17), calls=%async_computation.2 | async-start | bytes 3670016 | tf_op jit(solution)/shard_map/all_to_all | solution.py:14
  63.4 0.0 copy-start
  63.4 0.1 copy.16
  63.4 0.1 copy.17
  63.6 19.6 %all-to-all-done.2 = bf16[4,512,448]{1,2,0:T(8,128)(2,1)S(1)} async-done(((bf16[4,512,448]{1,2,0:T(8,128)(2,1)}), bf16[4,512,448]{1,2,0:T(8,128)(2,1)S(1)}, u32[]{:S(2)}, u32[]{:S(2)}) %all-to-all-start.2) | async-done | bytes 1835040 | tf_op jit(solution)/shard_map/all_to_all | solution.py:14
  83.2 22.1 %all_to_all.46 = bf16[16,32,512]{2,1,0:T(8,128)(2,1)S(1)} all-to-all(bf16[16,32,512]{2,1,0:T(8,128)(2,1)S(1)} %bitcast.49), channel_id=1, replica_groups=mesh['x'=4,'y'=4,'zh'=8,'zl'=4,'c'=2] {'x','zl'}, dimensions={0} | all-to-all | bytes 1048576 | tf_op jit(solution)/shard_map/all_to_all | solution.py:14
  105.3 0.0 copy-done
  105.3 1.4 broadcast_in_dim.18
  106.7 4.4 %all-to-all-start.3 = ((bf16[4,512,448]{1,2,0:T(8,128)(2,1)}), bf16[4,512,448]{1,2,0:T(8,128)(2,1)}, u32[]{:S(2)}, u32[]{:S(2)}) async-start(bf16[4,512,448]{1,2,0:T(8,128)(2,1)} %broadcast_in_dim.18), calls=%async_computation.3 | async-start | bytes 3670016 | tf_op jit(solution)/shard_map/all_to_all | solution.py:14
  111.1 1.9 collective-permute-start
  113.0 1.9 collective-permute-done
  114.9 0.1 pad_maximum_fusion
  115.0 1.4 fusion
  116.4 0.0 copy-start.2
  116.4 16.8 %all-to-all-done.3 = bf16[4,512,448]{1,2,0:T(8,128)(2,1)} async-done(((bf16[4,512,448]{1,2,0:T(8,128)(2,1)}), bf16[4,512,448]{1,2,0:T(8,128)(2,1)}, u32[]{:S(2)}, u32[]{:S(2)}) %all-to-all-start.3) | async-done | bytes 1835040 | tf_op jit(solution)/shard_map/all_to_all | solution.py:14
  133.1 2.2 fusion.1
  135.3 0.0 copy-done.2
  135.3 0.0 copy-start.1
  135.4 0.2 copy.19
  135.6 11.0 %all_to_all.47 = bf16[4,64,896]{2,1,0:T(8,128)(2,1)S(1)} all-to-all(bf16[4,64,896]{2,1,0:T(8,128)(2,1)S(1)} %bitcast.53), channel_id=1, replica_groups=mesh['x'=4,'y'=4,'zh'=8,'zl'=4,'c'=2] {'y'}, dimensions={0} | all-to-all | bytes 917504 | tf_op jit(solution)/shard_map/all_to_all | solution.py:14
  146.6 0.0 copy-done.1
  146.6 1.4 broadcast_in_dim.20
  148.0 3.6 %all-to-all-start.6 = ((bf16[4,448,512]{2,1,0:T(8,128)(2,1)}), bf16[4,448,512]{2,1,0:T(8,128)(2,1)S(1)}, u32[]{:S(2)}, u32[]{:S(2)}) async-start(bf16[4,448,512]{2,1,0:T(8,128)(2,1)} %broadcast_in_dim.20), calls=%async_computation.6 | async-start | bytes 3670016 | tf_op jit(solution)/shard_map/all_to_all | solution.py:14
  151.6 0.1 convert_reduce_fusion
  151.6 0.1 fusion.5
  151.8 19.4 %all-to-all-done.6 = bf16[4,448,512]{2,1,0:T(8,128)(2,1)S(1)} async-done(((bf16[4,448,512]{2,1,0:T(8,128)(2,1)}), bf16[4,448,512]{2,1,0:T(8,128)(2,1)S(1)}, u32[]{:S(2)}, u32[]{:S(2)}) %all-to-all-start.6) | async-done | bytes 1835040 | tf_op jit(solution)/shard_map/all_to_all | solution.py:14
  171.2 9.1 %all_to_all.48 = bf16[4,64,448]{2,1,0:T(8,128)(2,1)S(1)} all-to-all(bf16[4,64,448]{2,1,0:T(8,128)(2,1)S(1)} %broadcast_in_dim.19), channel_id=1, replica_groups=mesh['x'=4,'y'=4,'zh'=8,'zl'=4,'c'=2] {'y'}, dimensions={0} | all-to-all | bytes 458752 | tf_op jit(solution)/shard_map/all_to_all | solution.py:14
  180.3 0.7 fusion.6
  181.0 0.1 fusion.4
  181.0 1.9 collective-permute-start.1
  183.0 1.9 collective-permute-done.1
  184.8 0.2 fusion.3
  185.0 0.0 copy-start.3
  185.0 19.7 %all_to_all.49 = bf16[16,32,512]{2,1,0:T(8,128)(2,1)S(1)} all-to-all(bf16[16,32,512]{2,1,0:T(8,128)(2,1)S(1)} %bitcast.52), channel_id=1, replica_groups=mesh['x'=4,'y'=4,'zh'=8,'zl'=4,'c'=2] {'x','zl'}, dimensions={0} | all-to-all | bytes 1048576 | tf_op jit(solution)/shard_map/all_to_all | solution.py:14
  204.7 0.1 bitcast_reduce_fusion
  204.8 0.1 copy.22
  204.9 0.1 copy.23
  205.0 0.7 copy.24
  205.7 8.0 %all-to-all-start.8 = ((bf16[8,16,512]{2,1,0:T(8,128)(2,1)}), bf16[8,16,512]{2,1,0:T(8,128)(2,1)S(1)}, u32[]{:S(2)}, u32[]{:S(2)}) async-start(bf16[8,16,512]{2,1,0:T(8,128)(2,1)} %copy.24), calls=%async_computation.8 | async-start | bytes 262144 | tf_op jit(solution)/shard_map/all_to_all | solution.py:14
  213.7 0.0 copy-done.3
  213.7 27.8 %all-to-all-done.8 = bf16[8,16,512]{2,1,0:T(8,128)(2,1)S(1)} async-done(((bf16[8,16,512]{2,1,0:T(8,128)(2,1)}), bf16[8,16,512]{2,1,0:T(8,128)(2,1)S(1)}, u32[]{:S(2)}, u32[]{:S(2)}) %all-to-all-start.8) | async-done | bytes 131104 | tf_op jit(solution)/shard_map/all_to_all | solution.py:14
  241.6 0.7 multiply_convert_fusion
  (6 shorter events, 0.1 us)
Async XLA Ops:
  59.1 24.1 %all-to-all-start.2 = ((bf16[4,512,448]{1,2,0:T(8,128)(2,1)}), bf16[4,512,448]{1,2,0:T(8,128)(2,1)S(1)}, u32[]{:S(2)}, u32[]{:S(2)}) async-start(bf16[4,512,448]{1,2,0:T(8,128)(2,1)} %broadcast_in_dim.17), calls=%async_computation.2 | async-start | bytes 3670016 | tf_op jit(solution)/shard_map/all_to_all | solution.py:14
  63.4 42.0 %copy-start = (bf16[512,448]{0,1:T(8,128)(2,1)S(1)}, bf16[512,448]{0,1:T(8,128)(2,1)}, u32[]{:S(2)}) copy-start(bf16[512,448]{0,1:T(8,128)(2,1)} %param.8) | copy-start | bytes 1376260
  106.7 26.4 %all-to-all-start.3 = ((bf16[4,512,448]{1,2,0:T(8,128)(2,1)}), bf16[4,512,448]{1,2,0:T(8,128)(2,1)}, u32[]{:S(2)}, u32[]{:S(2)}) async-start(bf16[4,512,448]{1,2,0:T(8,128)(2,1)} %broadcast_in_dim.18), calls=%async_computation.3 | async-start | bytes 3670016 | tf_op jit(solution)/shard_map/all_to_all | solution.py:14
  111.1 3.8 %collective-permute-start = (bf16[4,4,1,32,512]{4,3,2,1,0:T(8,128)(2,1)S(1)}, bf16[4,4,1,32,512]{4,3,2,1,0:T(8,128)(2,1)S(1)}, u32[]{:S(2)}, u32[]{:S(2)}) collective-permute-start(bf16[4,4,1,32,512]{4,3,2,1,0:T(8,128)(2,1)S(1)} %bitcast.50), channel_id=1, source_target_pairs={{0,1},{1,0},{2,3},{3,2},{4,5},{5,4},{6,7},{7,6},{8,9},{9,8},{10,11... | collective-permute-start | bytes 1572872 | tf_op jit(solution)/shard_map/ppermute | solution.py:22
  116.4 18.9 %copy-start.2 = (bf16[256,448]{0,1:T(8,128)(2,1)S(1)}, bf16[256,448]{0,1:T(8,128)(2,1)}, u32[]{:S(2)}) copy-start(bf16[256,448]{0,1:T(8,128)(2,1)} %fusion) | copy-start | bytes 688132
  135.3 11.3 %copy-start.1 = (bf16[448,512]{1,0:T(8,128)(2,1)S(1)}, bf16[448,512]{1,0:T(8,128)(2,1)}, u32[]{:S(2)}) copy-start(bf16[448,512]{1,0:T(8,128)(2,1)} %param.9) | copy-start | bytes 1376260
  148.0 23.2 %all-to-all-start.6 = ((bf16[4,448,512]{2,1,0:T(8,128)(2,1)}), bf16[4,448,512]{2,1,0:T(8,128)(2,1)S(1)}, u32[]{:S(2)}, u32[]{:S(2)}) async-start(bf16[4,448,512]{2,1,0:T(8,128)(2,1)} %broadcast_in_dim.20), calls=%async_computation.6 | async-start | bytes 3670016 | tf_op jit(solution)/shard_map/all_to_all | solution.py:14
  181.0 3.8 %collective-permute-start.1 = (bf16[4,4,32,512]{3,2,1,0:T(8,128)(2,1)S(1)}, bf16[4,4,32,512]{3,2,1,0:T(8,128)(2,1)S(1)}, u32[]{:S(2)}, u32[]{:S(2)}) collective-permute-start(bf16[4,4,32,512]{3,2,1,0:T(8,128)(2,1)S(1)} %fusion.4), channel_id=1, source_target_pairs={{0,1},{1,0},{2,3},{3,2},{4,5},{5,4},{6,7},{7,6},{8,9},{9,8},{10,11... | collective-permute-start | bytes 1572872 | tf_op jit(solution)/shard_map/ppermute | solution.py:22
  185.0 28.7 %copy-start.3 = (s32[16]{0:T(128)S(1)}, s32[16]{0:T(128)}, u32[]{:S(2)}) copy-start(s32[16]{0:T(128)} %param.6) | copy-start | bytes 196
  205.7 35.9 %all-to-all-start.8 = ((bf16[8,16,512]{2,1,0:T(8,128)(2,1)}), bf16[8,16,512]{2,1,0:T(8,128)(2,1)S(1)}, u32[]{:S(2)}, u32[]{:S(2)}) async-start(bf16[8,16,512]{2,1,0:T(8,128)(2,1)} %copy.24), calls=%async_computation.8 | async-start | bytes 262144 | tf_op jit(solution)/shard_map/all_to_all | solution.py:14

commit v2 on v1

v2 whole, which is shorter than its diff:
```python
import jax
import jax.numpy as jnp
from jax import lax
from jax.experimental import pallas as pl
from jax.experimental.pallas import tpu as pltpu
from jax.sharding import Mesh, PartitionSpec as P

X, Y, ZH, ZL, C = 4, 4, 8, 4, 2
DP = ("zh", "zl", "c")
TENSOR = ("x", "y")
F32 = jnp.float32
BF16 = jnp.bfloat16
VMEM = pl.BlockSpec(memory_space=pltpu.VMEM)
PARAMS = pltpu.CompilerParams(vmem_limit_bytes=24 << 20)


def exchange(pieces, axes):
    return lax.all_to_all(pieces, axes, split_axis=0, concat_axis=0, tiled=True)


def spread(block, count, axes):
    return exchange(jnp.broadcast_to(block[None], (count,) + block.shape), axes)


def swap_cores(block):
    return lax.ppermute(block, "c", [(0, 1), (1, 0)])


def from_behind(block, step):
    return lax.ppermute(block, "x", [(i, (i + step) % X) for i in range(X)])


def behind(step):
    return lax.rem(lax.axis_index("x") + (X - step), X)


def first_kernel(own_ref, other_ref, *refs):
    weights, out_ref = refs[:-1], refs[-1]
    side, _, rows, columns = out_ref.shape
    total = None
    for step, pair_ref in enumerate(weights):
        block = behind(step)
        pair = pair_ref[...].reshape(columns, pair_ref.shape[2])
        both = jnp.concatenate([own_ref[block], other_ref[block]], axis=0)
        term = lax.dot_general(both, pair, (((1,), (1,)), ((), ())), preferred_element_type=F32)
        total = term if total is None else total + term
    total = total.astype(BF16).reshape(C, side, rows, columns)
    for core in range(C):
        out_ref[:, core] = total[core]


def first(own, other, weights):
    rows = own.shape[1] // ZL
    columns = 2 * weights[0].shape[1]
    return pl.pallas_call(
        first_kernel,
        out_shape=jax.ShapeDtypeStruct((ZL, C, rows, columns), BF16),
        in_specs=[VMEM] * (2 + X),
        out_specs=VMEM,
        compiler_params=PARAMS,
    )(own, other, *weights)


def second_kernel(hidden_ref, *refs):
    weights, own_ref, other_ref = refs[:-2], refs[-2], refs[-1]
    side, rows, width = hidden_ref.shape
    rows = rows // C
    mine = hidden_ref[:, :rows].reshape(side * rows, width)
    other = hidden_ref[:, rows:].reshape(side * rows, width)
    both = jnp.concatenate([mine, other], axis=0)
    for step, down_ref in enumerate(weights):
        part = jnp.dot(both, down_ref[...], preferred_element_type=F32)
        own_ref[behind(step)] = part[: side * rows]
        other_ref[behind(step)] = part[side * rows :].astype(BF16)


def second(hidden, weights):
    shape = (X, hidden.shape[0] * hidden.shape[1] // C, weights[0].shape[1])
    return pl.pallas_call(
        second_kernel,
        out_shape=(jax.ShapeDtypeStruct(shape, F32), jax.ShapeDtypeStruct(shape, BF16)),
        in_specs=[VMEM] * (1 + X),
        out_specs=(VMEM, VMEM),
        compiler_params=PARAMS,
    )(hidden, *weights)


def on_device(tokens, pad_mask, gate_weight, up_weight, down_weight):
    rows, feats = tokens.shape
    width = gate_weight.shape[1]
    sub = rows // X
    some = ZH * sub

    far = spread(tokens, ZH, "zh")
    pair = jnp.stack([gate_weight.T, up_weight.T])
    pairs = [pair, from_behind(pair, 1), None, from_behind(pair, 3)]
    far, pairs[1], pairs[3], down_weight = lax.optimization_barrier((far, pairs[1], pairs[3], down_weight))

    far = far.reshape(ZH, X, sub, feats).transpose(1, 0, 2, 3).reshape(X, 1, some, feats)
    far = jnp.broadcast_to(far, (X, ZL, some, feats)).reshape(X * ZL, some, feats)
    own = exchange(far, ("x", "zl")).reshape(X, ZL * some, feats)
    pairs[2] = from_behind(pair, 2)
    downs = [down_weight] + [from_behind(down_weight, step) for step in range(1, X)]
    own, pairs[2], downs[1] = lax.optimization_barrier((own, pairs[2], downs[1]))

    sums = first(own, swap_cores(own), pairs)
    sums, downs[3] = lax.optimization_barrier((sums, downs[3]))
    sums = exchange(sums.reshape(Y, C * some, 2 * width), "y")
    sums, downs[2] = lax.optimization_barrier((sums, downs[2]))
    sums = jnp.sum(sums.astype(F32), axis=0)
    gate, up = sums[:, :width], sums[:, width:]
    hidden = (gate * jax.nn.sigmoid(gate) * up).astype(BF16)
    hidden = spread(hidden, Y, "y")

    part, other = second(hidden, downs)
    part = (part + swap_cores(other).astype(F32)).astype(BF16)
    part = exchange(part.reshape(X * ZL, some, feats), ("x", "zl"))
    part = jnp.sum(part.reshape(X, ZL, some, feats).astype(F32), axis=1).astype(BF16)
    part = part.reshape(X, ZH, sub, feats).transpose(1, 0, 2, 3).reshape(ZH, rows, feats)
    result = jnp.sum(exchange(part, "zh").astype(F32), axis=0)
    return (result * pad_mask[:, None].astype(F32)).astype(BF16)


def solution(mesh):
    fine = Mesh(mesh.devices.reshape(X, Y, ZH, ZL, C), TENSOR + DP)
    placed = (P(DP, TENSOR), P(DP), P(TENSOR, DP), P(TENSOR, DP), P(DP, TENSOR))
    return jax.shard_map(
        on_device, mesh=fine, in_specs=placed, out_specs=P(DP, TENSOR), check_vma=False
    )
```

time: 243 us -> 213 us (0.88)
  the two profiles are of different devices: /device:TPU:8 before, /device:TPU:64 now
where the time goes in v2:
time: 213 us
  waiting for transfers between devices  104 us (49%)
  starting transfers between devices  67.8 us (32%)
  blocking collectives  28.5 us (13%)
  local copies, waits for them, and re-layouts  6.28 us (3%)
  Pallas kernels  3.77 us (2%)
  other arithmetic  2.36 us (1%)
    all_to_all x4, waiting for transfers between devices, exchange(): return lax.all_to_all(pieces, axes, split_axis=0, concat_axis=0, tiled=True)  67.9 us
    all_to_all x4, starting transfers between devices, exchange(): return lax.all_to_all(pieces, axes, split_axis=0, concat_axis=0, tiled=True)  43.2 us
    ppermute x6, waiting for transfers between devices, from_behind(): return lax.ppermute(block, 'x', [(i, (i + step) % X) for i in range(X)])  34 us
    all_to_all x2, blocking collectives, exchange(): return lax.all_to_all(pieces, axes, split_axis=0, concat_axis=0, tiled=True)  28.5 us
    ppermute x6, starting transfers between devices, from_behind(): return lax.ppermute(block, 'x', [(i, (i + step) % X) for i in range(X)])  20.7 us
  transfers between devices with their start and end apart: 12, of which 7 were waited for; matrix products, arithmetic and copies ran while one was open for 0% of the time, Pallas kernels for 1%

profile of v2, /device:TPU:64, one launch (start us, length us, event | category | flops | bytes accessed | tf_op | source)
XLA Modules:
  0.0 212.6 jit_solution(11217719111489758060)
XLA Ops:
  0.0 0.0 copy-start.7
  0.0 1.3 pad_maximum_fusion.refs_0_
  1.3 3.4 %collective-permute-start = (bf16[2,448,512]{2,1,0:T(8,128)(2,1)S(1)}, bf16[2,448,512]{2,1,0:T(8,128)(2,1)S(1)}, u32[]{:S(2)}, u32[]{:S(2)}) collective-permute-start(bf16[2,448,512]{2,1,0:T(8,128)(2,1)S(1)} %pad_maximum_fusion.refs_0_), channel_id=1, source_target_pairs={{0,256},{256,512},{512,768},{768,0},{1,257},{257,513},{513,769},{7... | collective-permute-start | bytes 2752520 | tf_op jit(solution)/shard_map/ppermute | solution.py:30
  4.7 3.7 %collective-permute-start.1 = (bf16[2,448,512]{2,1,0:T(8,128)(2,1)S(1)}, bf16[2,448,512]{2,1,0:T(8,128)(2,1)S(1)}, u32[]{:S(2)}, u32[]{:S(2)}) collective-permute-start(bf16[2,448,512]{2,1,0:T(8,128)(2,1)S(1)} %pad_maximum_fusion.refs_0_), channel_id=1, source_target_pairs={{0,768},{256,0},{512,256},{768,512},{1,769},{257,1},{513,257},{769... | collective-permute-start | bytes 2752520 | tf_op jit(solution)/shard_map/ppermute | solution.py:30
  8.3 0.0 copy-done.7
  8.3 0.7 broadcast_in_dim.8
  9.0 26.5 %all-to-all-start = ((bf16[8,16,512]{2,1,0:T(8,128)(2,1)}), bf16[8,16,512]{2,1,0:T(8,128)(2,1)S(1)}, u32[]{:S(2)}, u32[]{:S(2)}) async-start(bf16[8,16,512]{2,1,0:T(8,128)(2,1)} %broadcast_in_dim.8), calls=%async_computation | async-start | bytes 262144 | tf_op jit(solution)/shard_map/all_to_all | solution.py:18
  35.5 0.0 collective-permute-done.refs_1_
  35.6 0.0 collective-permute-done.1.refs_3_
  35.6 29.5 %all-to-all-done = bf16[8,16,512]{2,1,0:T(8,128)(2,1)S(1)} async-done(((bf16[8,16,512]{2,1,0:T(8,128)(2,1)}), bf16[8,16,512]{2,1,0:T(8,128)(2,1)S(1)}, u32[]{:S(2)}, u32[]{:S(2)}) %all-to-all-start) | async-done | bytes 131104 | tf_op jit(solution)/shard_map/all_to_all | solution.py:18
  65.1 0.1 copy.9
  65.2 0.1 copy.10
  65.3 0.9 broadcast_in_dim.10
  66.2 5.5 %all-to-all-start.1 = ((bf16[16,32,512]{2,1,0:T(8,128)(2,1)}), bf16[16,32,512]{2,1,0:T(8,128)(2,1)S(1)}, u32[]{:S(2)}, u32[]{:S(2)}) async-start(bf16[16,32,512]{2,1,0:T(8,128)(2,1)} %bitcast.22), calls=%async_computation.1 | async-start | bytes 1048576 | tf_op jit(solution)/shard_map/all_to_all | solution.py:18
  71.6 4.9 %collective-permute-start.2 = (bf16[2,448,512]{2,1,0:T(8,128)(2,1)S(1)}, bf16[2,448,512]{2,1,0:T(8,128)(2,1)S(1)}, u32[]{:S(2)}, u32[]{:S(2)}) collective-permute-start(bf16[2,448,512]{2,1,0:T(8,128)(2,1)S(1)} %pad_maximum_fusion.refs_0_), channel_id=1, source_target_pairs={{0,512},{256,768},{512,0},{768,256},{1,513},{257,769},{513,1},{769... | collective-permute-start | bytes 2752520 | tf_op jit(solution)/shard_map/ppermute | solution.py:30
  76.5 2.5 %collective-permute-start.3 = (bf16[448,512]{1,0:T(8,128)(2,1)}, bf16[448,512]{1,0:T(8,128)(2,1)S(1)}, u32[]{:S(2)}, u32[]{:S(2)}) collective-permute-start(bf16[448,512]{1,0:T(8,128)(2,1)} %refs_0_), channel_id=1, source_target_pairs={{0,256},{256,512},{512,768},{768,0},{1,257},{257,513},{513,769},{7... | collective-permute-start | bytes 1376264 | tf_op jit(solution)/shard_map/ppermute | solution.py:30
  79.0 21.3 %collective-permute-done.2.refs_2_ = bf16[2,448,512]{2,1,0:T(8,128)(2,1)S(1)} collective-permute-done((bf16[2,448,512]{2,1,0:T(8,128)(2,1)S(1)}, bf16[2,448,512]{2,1,0:T(8,128)(2,1)S(1)}, u32[]{:S(2)}, u32[]{:S(2)}) %collective-permute-start.2) | collective-permute-done | bytes 917536 | tf_op jit(solution)/shard_map/ppermute | solution.py:30
  100.3 0.0 copy-start
  100.3 0.9 copy-done
  101.2 6.8 %collective-permute-done.3.refs_1_ = bf16[448,512]{1,0:T(8,128)(2,1)S(1)} collective-permute-done((bf16[448,512]{1,0:T(8,128)(2,1)}, bf16[448,512]{1,0:T(8,128)(2,1)S(1)}, u32[]{:S(2)}, u32[]{:S(2)}) %collective-permute-start.3) | collective-permute-done | bytes 458784 | tf_op jit(solution)/shard_map/ppermute | solution.py:30
  108.0 0.0 copy-start.3
  108.0 0.8 copy-done.3
  108.8 0.0 all-to-all-done.1
  108.8 2.0 collective-permute-start.4
  110.7 2.4 %collective-permute-start.5 = (bf16[448,512]{1,0:T(8,128)(2,1)}, bf16[448,512]{1,0:T(8,128)(2,1)S(1)}, u32[]{:S(2)}, u32[]{:S(2)}) collective-permute-start(bf16[448,512]{1,0:T(8,128)(2,1)} %refs_0_), channel_id=1, source_target_pairs={{0,768},{256,0},{512,256},{768,512},{1,769},{257,1},{513,257},{769... | collective-permute-start | bytes 1376264 | tf_op jit(solution)/shard_map/ppermute | solution.py:30
  113.2 3.9 %collective-permute-start.6 = (bf16[448,512]{1,0:T(8,128)(2,1)}, bf16[448,512]{1,0:T(8,128)(2,1)}, u32[]{:S(2)}, u32[]{:S(2)}) collective-permute-start(bf16[448,512]{1,0:T(8,128)(2,1)} %refs_0_), channel_id=1, source_target_pairs={{0,512},{256,768},{512,0},{768,256},{1,513},{257,769},{513,1},{769... | collective-permute-start | bytes 1376264 | tf_op jit(solution)/shard_map/ppermute | solution.py:30
  117.1 0.0 collective-permute-done.4.other_ref
  117.1 0.0 copy-start.1
  117.1 1.2 copy-done.1
  118.2 2.0 shard_map.55
  120.3 5.9 %collective-permute-done.5.refs_3_ = bf16[448,512]{1,0:T(8,128)(2,1)S(1)} collective-permute-done((bf16[448,512]{1,0:T(8,128)(2,1)}, bf16[448,512]{1,0:T(8,128)(2,1)S(1)}, u32[]{:S(2)}, u32[]{:S(2)}) %collective-permute-start.5) | collective-permute-done | bytes 458784 | tf_op jit(solution)/shard_map/ppermute | solution.py:30
  126.2 0.0 copy-start.5
  126.2 0.8 copy-done.5
  126.9 4.5 %all-to-all-start.2 = ((bf16[4,64,896]{2,1,0:T(8,128)(2,1)}), bf16[4,64,896]{2,1,0:T(8,128)(2,1)S(1)}, u32[]{:S(2)}, u32[]{:S(2)}) async-start(bf16[4,64,896]{2,1,0:T(8,128)(2,1)} %bitcast.9), calls=%async_computation.2 | async-start | bytes 917504 | tf_op jit(solution)/shard_map/all_to_all | solution.py:18
  131.4 0.0 collective-permute-done.6.refs_2_
  131.4 8.3 %all-to-all-done.2 = bf16[4,64,896]{2,1,0:T(8,128)(2,1)S(1)} async-done(((bf16[4,64,896]{2,1,0:T(8,128)(2,1)}), bf16[4,64,896]{2,1,0:T(8,128)(2,1)S(1)}, u32[]{:S(2)}, u32[]{:S(2)}) %all-to-all-start.2) | async-done | bytes 458784 | tf_op jit(solution)/shard_map/all_to_all | solution.py:18
  139.7 0.0 copy-start.6
  139.7 0.1 convert_reduce_fusion
  139.7 0.0 copy-start.4
  139.7 0.1 fusion
  139.8 0.0 copy-start.2
  139.9 9.2 %all_to_all.30.hidden_ref = bf16[4,64,448]{2,1,0:T(8,128)(2,1)S(1)} all-to-all(bf16[4,64,448]{2,1,0:T(8,128)(2,1)S(1)} %broadcast_in_dim.11), channel_id=1, replica_groups=mesh['x'=4,'y'=4,'zh'=8,'zl'=4,'c'=2] {'y'}, dimensions={0} | all-to-all | bytes 458752 | tf_op jit(solution)/shard_map/all_to_all | solution.py:18
  149.1 0.0 copy-done.6
  149.1 0.0 copy-done.4
  149.1 0.0 copy-done.2
  149.1 1.7 shard_map.56
  150.8 1.9 collective-permute-start.7
  152.7 1.9 collective-permute-done.7
  154.6 0.2 add_convert_fusion
  154.8 19.3 %all_to_all.31 = bf16[16,32,512]{2,1,0:T(8,128)(2,1)S(1)} all-to-all(bf16[16,32,512]{2,1,0:T(8,128)(2,1)S(1)} %bitcast.23), channel_id=1, replica_groups=mesh['x'=4,'y'=4,'zh'=8,'zl'=4,'c'=2] {'x','zl'}, dimensions={0} | all-to-all | bytes 1048576 | tf_op jit(solution)/shard_map/all_to_all | solution.py:18
  174.1 0.1 bitcast_reduce_fusion
  174.1 0.1 copy.12
  174.3 0.1 copy.13
  174.3 0.7 copy.14
  175.0 0.0 copy-start.8
  175.0 6.7 %all-to-all-start.5 = ((bf16[8,16,512]{2,1,0:T(8,128)(2,1)}), bf16[8,16,512]{2,1,0:T(8,128)(2,1)S(1)}, u32[]{:S(2)}, u32[]{:S(2)}) async-start(bf16[8,16,512]{2,1,0:T(8,128)(2,1)} %copy.14), calls=%async_computation.5 | async-start | bytes 262144 | tf_op jit(solution)/shard_map/all_to_all | solution.py:18
  181.7 0.0 copy-done.8
  181.8 30.2 %all-to-all-done.5 = bf16[8,16,512]{2,1,0:T(8,128)(2,1)S(1)} async-done(((bf16[8,16,512]{2,1,0:T(8,128)(2,1)}), bf16[8,16,512]{2,1,0:T(8,128)(2,1)S(1)}, u32[]{:S(2)}, u32[]{:S(2)}) %all-to-all-start.5) | async-done | bytes 131104 | tf_op jit(solution)/shard_map/all_to_all | solution.py:18
  211.9 0.7 multiply_convert_fusion
  (4 shorter events, 0.1 us)
Async XLA Ops:
  0.0 8.3 %copy-start.7 = (bf16[16,512]{1,0:T(8,128)(2,1)S(1)}, bf16[16,512]{1,0:T(8,128)(2,1)}, u32[]{:S(2)}) copy-start(bf16[16,512]{1,0:T(8,128)(2,1)} %param.5) | copy-start | bytes 49156
  1.3 34.3 %collective-permute-start = (bf16[2,448,512]{2,1,0:T(8,128)(2,1)S(1)}, bf16[2,448,512]{2,1,0:T(8,128)(2,1)S(1)}, u32[]{:S(2)}, u32[]{:S(2)}) collective-permute-start(bf16[2,448,512]{2,1,0:T(8,128)(2,1)S(1)} %pad_maximum_fusion.refs_0_), channel_id=1, source_target_pairs={{0,256},{256,512},{512,768},{768,0},{1,257},{257,513},{513,769},{7... | collective-permute-start | bytes 2752520 | tf_op jit(solution)/shard_map/ppermute | solution.py:30
  4.7 30.9 %collective-permute-start.1 = (bf16[2,448,512]{2,1,0:T(8,128)(2,1)S(1)}, bf16[2,448,512]{2,1,0:T(8,128)(2,1)S(1)}, u32[]{:S(2)}, u32[]{:S(2)}) collective-permute-start(bf16[2,448,512]{2,1,0:T(8,128)(2,1)S(1)} %pad_maximum_fusion.refs_0_), channel_id=1, source_target_pairs={{0,768},{256,0},{512,256},{768,512},{1,769},{257,1},{513,257},{769... | collective-permute-start | bytes 2752520 | tf_op jit(solution)/shard_map/ppermute | solution.py:30
  9.0 56.1 %all-to-all-start = ((bf16[8,16,512]{2,1,0:T(8,128)(2,1)}), bf16[8,16,512]{2,1,0:T(8,128)(2,1)S(1)}, u32[]{:S(2)}, u32[]{:S(2)}) async-start(bf16[8,16,512]{2,1,0:T(8,128)(2,1)} %broadcast_in_dim.8), calls=%async_computation | async-start | bytes 262144 | tf_op jit(solution)/shard_map/all_to_all | solution.py:18
  66.2 42.6 %all-to-all-start.1 = ((bf16[16,32,512]{2,1,0:T(8,128)(2,1)}), bf16[16,32,512]{2,1,0:T(8,128)(2,1)S(1)}, u32[]{:S(2)}, u32[]{:S(2)}) async-start(bf16[16,32,512]{2,1,0:T(8,128)(2,1)} %bitcast.22), calls=%async_computation.1 | async-start | bytes 1048576 | tf_op jit(solution)/shard_map/all_to_all | solution.py:18
  71.6 28.7 %collective-permute-start.2 = (bf16[2,448,512]{2,1,0:T(8,128)(2,1)S(1)}, bf16[2,448,512]{2,1,0:T(8,128)(2,1)S(1)}, u32[]{:S(2)}, u32[]{:S(2)}) collective-permute-start(bf16[2,448,512]{2,1,0:T(8,128)(2,1)S(1)} %pad_maximum_fusion.refs_0_), channel_id=1, source_target_pairs={{0,512},{256,768},{512,0},{768,256},{1,513},{257,769},{513,1},{769... | collective-permute-start | bytes 2752520 | tf_op jit(solution)/shard_map/ppermute | solution.py:30
  76.5 31.5 %collective-permute-start.3 = (bf16[448,512]{1,0:T(8,128)(2,1)}, bf16[448,512]{1,0:T(8,128)(2,1)S(1)}, u32[]{:S(2)}, u32[]{:S(2)}) collective-permute-start(bf16[448,512]{1,0:T(8,128)(2,1)} %refs_0_), channel_id=1, source_target_pairs={{0,256},{256,512},{512,768},{768,0},{1,257},{257,513},{513,769},{7... | collective-permute-start | bytes 1376264 | tf_op jit(solution)/shard_map/ppermute | solution.py:30
  100.3 0.9 copy-start
  108.0 0.8 copy-start.3
  108.8 8.3 %collective-permute-start.4 = (bf16[4,128,512]{2,1,0:T(8,128)(2,1)S(1)}, bf16[4,128,512]{2,1,0:T(8,128)(2,1)S(1)}, u32[]{:S(2)}, u32[]{:S(2)}) collective-permute-start(bf16[4,128,512]{2,1,0:T(8,128)(2,1)S(1)} %bitcast.20), channel_id=1, source_target_pairs={{0,1},{1,0},{2,3},{3,2},{4,5},{5,4},{6,7},{7,6},{8,9},{9,8},{10,11... | collective-permute-start | bytes 1572872 | tf_op jit(solution)/shard_map/ppermute | solution.py:26
  110.7 15.4 %collective-permute-start.5 = (bf16[448,512]{1,0:T(8,128)(2,1)}, bf16[448,512]{1,0:T(8,128)(2,1)S(1)}, u32[]{:S(2)}, u32[]{:S(2)}) collective-permute-start(bf16[448,512]{1,0:T(8,128)(2,1)} %refs_0_), channel_id=1, source_target_pairs={{0,768},{256,0},{512,256},{768,512},{1,769},{257,1},{513,257},{769... | collective-permute-start | bytes 1376264 | tf_op jit(solution)/shard_map/ppermute | solution.py:30
  113.2 18.2 %collective-permute-start.6 = (bf16[448,512]{1,0:T(8,128)(2,1)}, bf16[448,512]{1,0:T(8,128)(2,1)}, u32[]{:S(2)}, u32[]{:S(2)}) collective-permute-start(bf16[448,512]{1,0:T(8,128)(2,1)} %refs_0_), channel_id=1, source_target_pairs={{0,512},{256,768},{512,0},{768,256},{1,513},{257,769},{513,1},{769... | collective-permute-start | bytes 1376264 | tf_op jit(solution)/shard_map/ppermute | solution.py:30
  117.1 1.2 copy-start.1
  126.2 0.8 copy-start.5
  126.9 12.7 %all-to-all-start.2 = ((bf16[4,64,896]{2,1,0:T(8,128)(2,1)}), bf16[4,64,896]{2,1,0:T(8,128)(2,1)S(1)}, u32[]{:S(2)}, u32[]{:S(2)}) async-start(bf16[4,64,896]{2,1,0:T(8,128)(2,1)} %bitcast.9), calls=%async_computation.2 | async-start | bytes 917504 | tf_op jit(solution)/shard_map/all_to_all | solution.py:18
  139.7 9.4 %copy-start.6 = (bf16[448,512]{1,0:T(8,128)(2,1)S(1)}, bf16[448,512]{1,0:T(8,128)(2,1)}, u32[]{:S(2)}) copy-start(bf16[448,512]{1,0:T(8,128)(2,1)} %copy-done.5) | copy-start | bytes 1376260
  139.7 9.4 %copy-start.4 = (bf16[448,512]{1,0:T(8,128)(2,1)S(1)}, bf16[448,512]{1,0:T(8,128)(2,1)}, u32[]{:S(2)}) copy-start(bf16[448,512]{1,0:T(8,128)(2,1)} %copy-done.3) | copy-start | bytes 1376260
  139.8 9.2 %copy-start.2 = (bf16[448,512]{1,0:T(8,128)(2,1)S(1)}, bf16[448,512]{1,0:T(8,128)(2,1)}, u32[]{:S(2)}) copy-start(bf16[448,512]{1,0:T(8,128)(2,1)} %refs_0_) | copy-start | bytes 1376260
  150.8 3.8 %collective-permute-start.7 = (bf16[4,128,512]{2,1,0:T(8,128)(2,1)S(1)}, bf16[4,128,512]{2,1,0:T(8,128)(2,1)S(1)}, u32[]{:S(2)}, u32[]{:S(2)}) collective-permute-start(bf16[4,128,512]{2,1,0:T(8,128)(2,1)S(1)} %get-tuple-element.30), channel_id=1, source_target_pairs={{0,1},{1,0},{2,3},{3,2},{4,5},{5,4},{6,7},{7,6},{8,9},{9,8},{10,11... | collective-permute-start | bytes 1572872 | tf_op jit(solution)/shard_map/ppermute | solution.py:26
  175.0 6.7 %copy-start.8 = (s32[16]{0:T(128)S(1)}, s32[16]{0:T(128)}, u32[]{:S(2)}) copy-start(s32[16]{0:T(128)} %param.6) | copy-start | bytes 196
  175.0 36.9 %all-to-all-start.5 = ((bf16[8,16,512]{2,1,0:T(8,128)(2,1)}), bf16[8,16,512]{2,1,0:T(8,128)(2,1)S(1)}, u32[]{:S(2)}, u32[]{:S(2)}) async-start(bf16[8,16,512]{2,1,0:T(8,128)(2,1)} %copy.14), calls=%async_computation.5 | async-start | bytes 262144 | tf_op jit(solution)/shard_map/all_to_all | solution.py:18

commit v3 on v2

--- a/solution.py
+++ b/solution.py
@@ -10,6 +10,7 @@
 TENSOR = ("x", "y")
 F32 = jnp.float32
 BF16 = jnp.bfloat16
+STEPS = (0, 1, X - 1, 2)
 VMEM = pl.BlockSpec(memory_space=pltpu.VMEM)
 PARAMS = pltpu.CompilerParams(vmem_limit_bytes=24 << 20)
 
@@ -37,11 +38,14 @@
 def first_kernel(own_ref, other_ref, *refs):
     weights, out_ref = refs[:-1], refs[-1]
     side, _, rows, columns = out_ref.shape
+    feats = own_ref.shape[3]
+    pairs = [ref[...].reshape(columns, feats) for ref in weights[:3]]
+    pairs.append(jnp.concatenate([ref[...] for ref in weights[3:]], axis=0))
     total = None
-    for step, pair_ref in enumerate(weights):
+    for step, pair in zip(STEPS, pairs):
         block = behind(step)
-        pair = pair_ref[...].reshape(columns, pair_ref.shape[2])
-        both = jnp.concatenate([own_ref[block], other_ref[block]], axis=0)
+        both = [ref[:, block].reshape(side * rows, feats) for ref in (own_ref, other_ref)]
+        both = jnp.concatenate(both, axis=0)
         term = lax.dot_general(both, pair, (((1,), (1,)), ((), ())), preferred_element_type=F32)
         total = term if total is None else total + term
     total = total.astype(BF16).reshape(C, side, rows, columns)
@@ -50,12 +54,12 @@
 
 
 def first(own, other, weights):
-    rows = own.shape[1] // ZL
+    rows = own.shape[2]
     columns = 2 * weights[0].shape[1]
     return pl.pallas_call(
         first_kernel,
         out_shape=jax.ShapeDtypeStruct((ZL, C, rows, columns), BF16),
-        in_specs=[VMEM] * (2 + X),
+        in_specs=[VMEM] * (2 + len(weights)),
         out_specs=VMEM,
         compiler_params=PARAMS,
     )(own, other, *weights)
@@ -68,8 +72,10 @@
     mine = hidden_ref[:, :rows].reshape(side * rows, width)
     other = hidden_ref[:, rows:].reshape(side * rows, width)
     both = jnp.concatenate([mine, other], axis=0)
-    for step, down_ref in enumerate(weights):
-        part = jnp.dot(both, down_ref[...], preferred_element_type=F32)
+    downs = [ref[...] for ref in weights[:3]]
+    downs.append(jnp.concatenate([ref[...] for ref in weights[3:]], axis=0))
+    for step, down in zip(STEPS, downs):
+        part = jnp.dot(both, down, preferred_element_type=F32)
         own_ref[behind(step)] = part[: side * rows]
         other_ref[behind(step)] = part[side * rows :].astype(BF16)
 
@@ -79,7 +85,7 @@
     return pl.pallas_call(
         second_kernel,
         out_shape=(jax.ShapeDtypeStruct(shape, F32), jax.ShapeDtypeStruct(shape, BF16)),
-        in_specs=[VMEM] * (1 + X),
+        in_specs=[VMEM] * (1 + len(weights)),
         out_specs=(VMEM, VMEM),
         compiler_params=PARAMS,
     )(hidden, *weights)
@@ -90,23 +96,24 @@
     width = gate_weight.shape[1]
     sub = rows // X
     some = ZH * sub
+    half = down_weight.shape[0] // 32 * 16
 
-    far = spread(tokens, ZH, "zh")
     pair = jnp.stack([gate_weight.T, up_weight.T])
-    pairs = [pair, from_behind(pair, 1), None, from_behind(pair, 3)]
-    far, pairs[1], pairs[3], down_weight = lax.optimization_barrier((far, pairs[1], pairs[3], down_weight))
+    pairs = [pair, from_behind(pair, 1), from_behind(pair, X - 1)]
+    split = exchange(tokens.reshape(X, sub, feats), "x")
+    far = spread(split, ZH, "zh")
+    pairs += [from_behind(pairs[1][0], 1), from_behind(pairs[2][1], X - 1)]
+    far, down_weight, *pairs[3:] = lax.optimization_barrier((far, down_weight, *pairs[3:]))
 
-    far = far.reshape(ZH, X, sub, feats).transpose(1, 0, 2, 3).reshape(X, 1, some, feats)
-    far = jnp.broadcast_to(far, (X, ZL, some, feats)).reshape(X * ZL, some, feats)
-    own = exchange(far, ("x", "zl")).reshape(X, ZL * some, feats)
-    pairs[2] = from_behind(pair, 2)
-    downs = [down_weight] + [from_behind(down_weight, step) for step in range(1, X)]
-    own, pairs[2], downs[1] = lax.optimization_barrier((own, pairs[2], downs[1]))
+    far = far.transpose(1, 0, 2, 3).reshape(X, some, feats)
+    own = spread(far, ZL, "zl")
+    downs = [down_weight, from_behind(down_weight, 1), from_behind(down_weight, X - 1)]
+    own, downs[1], downs[2] = lax.optimization_barrier((own, downs[1], downs[2]))
+    downs += [from_behind(downs[1][:half], 1), from_behind(downs[2][half:], X - 1)]
 
     sums = first(own, swap_cores(own), pairs)
-    sums, downs[3] = lax.optimization_barrier((sums, downs[3]))
     sums = exchange(sums.reshape(Y, C * some, 2 * width), "y")
-    sums, downs[2] = lax.optimization_barrier((sums, downs[2]))
+    sums, *downs[3:] = lax.optimization_barrier((sums, *downs[3:]))
     sums = jnp.sum(sums.astype(F32), axis=0)
     gate, up = sums[:, :width], sums[:, width:]
     hidden = (gate * jax.nn.sigmoid(gate) * up).astype(BF16)

time: 213 us -> 212 us (level)
  waiting for transfers between devices: 104 us -> 66.3 us
  blocking collectives: 28.5 us -> 52.9 us
  starting transfers between devices: 67.8 us -> 77.4 us
    all_to_all x2 -> x3, blocking collectives: 28.5 us -> 52.9 us  [exchange(): return lax.all_to_all(pieces, axes, split_axis=0, concat_axis=0, tiled=True)]
    ppermute x6 -> x8, waiting for transfers between devices: 34 us -> 11.4 us  [from_behind(): return lax.ppermute(block, 'x', [(i, (i + step) % X) for i in range(X)])]
    all_to_all x4, waiting for transfers between devices: 67.9 us -> 51.2 us  [exchange(): return lax.all_to_all(pieces, axes, split_axis=0, concat_axis=0, tiled=True)]
    ppermute x6 -> x8, starting transfers between devices: 20.7 us -> 28.2 us  [from_behind(): return lax.ppermute(block, 'x', [(i, (i + step) % X) for i in range(X)])]
    all_to_all x4, starting transfers between devices: 43.2 us -> 45.4 us  [exchange(): return lax.all_to_all(pieces, axes, split_axis=0, concat_axis=0, tiled=True)]
  transfers between devices with their start and end apart: 12 -> 14, of which waited for: 7 -> 8; matrix products, arithmetic and copies ran while one was open for 0% -> 2% of each run, Pallas kernels for 1% -> 0%
where the time goes in v3:
time: 212 us; the launch traced here: 211 us
  starting transfers between devices  77.4 us (37%)
  waiting for transfers between devices  66.3 us (31%)
  blocking collectives  52.9 us (25%)
  local copies, waits for them, and re-layouts  7.73 us (4%)
  Pallas kernels  4.01 us (2%)
  other arithmetic  2.36 us (1%)
    all_to_all x3, blocking collectives, exchange(): return lax.all_to_all(pieces, axes, split_axis=0, concat_axis=0, tiled=True)  52.9 us
    all_to_all x4, waiting for transfers between devices, exchange(): return lax.all_to_all(pieces, axes, split_axis=0, concat_axis=0, tiled=True)  51.2 us
    all_to_all x4, starting transfers between devices, exchange(): return lax.all_to_all(pieces, axes, split_axis=0, concat_axis=0, tiled=True)  45.4 us
    ppermute x8, starting transfers between devices, from_behind(): return lax.ppermute(block, 'x', [(i, (i + step) % X) for i in range(X)])  28.2 us
    ppermute x8, waiting for transfers between devices, from_behind(): return lax.ppermute(block, 'x', [(i, (i + step) % X) for i in range(X)])  11.4 us
  transfers between devices with their start and end apart: 14, of which 8 were waited for; matrix products, arithmetic and copies ran while one was open for 2% of the time, Pallas kernels for 0%

profile of v3, /device:TPU:64, one launch (start us, length us, event | category | flops | bytes accessed | tf_op | source)
XLA Modules:
  0.0 210.9 jit_solution(8865714186057082962)
XLA Ops:
  0.0 0.0 copy-start.6
  0.0 1.3 pad_maximum_fusion.refs_0_
  1.3 3.4 %collective-permute-start = (bf16[2,448,512]{2,1,0:T(8,128)(2,1)S(1)}, bf16[2,448,512]{2,1,0:T(8,128)(2,1)S(1)}, u32[]{:S(2)}, u32[]{:S(2)}) collective-permute-start(bf16[2,448,512]{2,1,0:T(8,128)(2,1)S(1)} %pad_maximum_fusion.refs_0_), channel_id=1, source_target_pairs={{0,256},{256,512},{512,768},{768,0},{1,257},{257,513},{513,769},{7... | collective-permute-start | bytes 2752520 | tf_op jit(solution)/shard_map/ppermute | solution.py:31
  4.7 3.7 %collective-permute-start.2 = (bf16[2,448,512]{2,1,0:T(8,128)(2,1)S(1)}, bf16[2,448,512]{2,1,0:T(8,128)(2,1)S(1)}, u32[]{:S(2)}, u32[]{:S(2)}) collective-permute-start(bf16[2,448,512]{2,1,0:T(8,128)(2,1)S(1)} %pad_maximum_fusion.refs_0_), channel_id=1, source_target_pairs={{0,768},{256,0},{512,256},{768,512},{1,769},{257,1},{513,257},{769... | collective-permute-start | bytes 2752520 | tf_op jit(solution)/shard_map/ppermute | solution.py:31
  8.3 0.0 copy-done.6
  8.4 20.1 %all_to_all.35 = bf16[4,4,512]{2,1,0:T(4,128)(2,1)S(1)} all-to-all(bf16[4,4,512]{2,1,0:T(4,128)(2,1)S(1)} %reshape.23), channel_id=1, replica_groups=mesh['x'=4,'y'=4,'zh'=8,'zl'=4,'c'=2] {'x'}, dimensions={0} | all-to-all | bytes 32768 | tf_op jit(solution)/shard_map/all_to_all | solution.py:19
  28.5 0.7 broadcast_in_dim.8
  29.2 26.5 %all-to-all-start.1 = ((bf16[8,4,4,512]{3,2,1,0:T(4,128)(2,1)}), bf16[8,4,4,512]{3,2,1,0:T(4,128)(2,1)S(1)}, u32[]{:S(2)}, u32[]{:S(2)}) async-start(bf16[8,4,4,512]{3,2,1,0:T(4,128)(2,1)} %broadcast_in_dim.8), calls=%async_computation.1 | async-start | bytes 262144 | tf_op jit(solution)/shard_map/all_to_all | solution.py:19
  55.7 0.0 collective-permute-done.refs_1_
  55.7 0.8 slice_bitcast_fusion.1
  56.5 4.1 %collective-permute-start.1 = (bf16[448,512]{1,0:T(8,128)(2,1)}, bf16[448,512]{1,0:T(8,128)(2,1)S(1)}, u32[]{:S(2)}, u32[]{:S(2)}) collective-permute-start(bf16[448,512]{1,0:T(8,128)(2,1)} %slice_bitcast_fusion.1), channel_id=1, source_target_pairs={{0,256},{256,512},{512,768},{768,0},{1,257},{257,513},{513,769},{7... | collective-permute-start | bytes 1376264 | tf_op jit(solution)/shard_map/ppermute | solution.py:31
  60.6 0.0 collective-permute-done.2.refs_2_
  60.6 0.8 slice_bitcast_fusion
  61.5 3.0 %collective-permute-start.3 = (bf16[448,512]{1,0:T(8,128)(2,1)}, bf16[448,512]{1,0:T(8,128)(2,1)}, u32[]{:S(2)}, u32[]{:S(2)}) collective-permute-start(bf16[448,512]{1,0:T(8,128)(2,1)} %slice_bitcast_fusion), channel_id=1, source_target_pairs={{0,768},{256,0},{512,256},{768,512},{1,769},{257,1},{513,257},{769... | collective-permute-start | bytes 1376264 | tf_op jit(solution)/shard_map/ppermute | solution.py:31
  64.4 21.0 %all-to-all-done.1 = bf16[8,4,4,512]{3,2,1,0:T(4,128)(2,1)S(1)} async-done(((bf16[8,4,4,512]{3,2,1,0:T(4,128)(2,1)}), bf16[8,4,4,512]{3,2,1,0:T(4,128)(2,1)S(1)}, u32[]{:S(2)}, u32[]{:S(2)}) %all-to-all-start.1) | async-done | bytes 131104 | tf_op jit(solution)/shard_map/all_to_all | solution.py:19
  85.5 0.0 collective-permute-done.1.refs_3_
  85.5 0.0 copy-start.3
  85.5 0.0 collective-permute-done.3.refs_4_
  85.5 0.1 copy.10
  85.6 0.9 broadcast_in_dim.10
  86.4 0.0 copy-done.3
  86.4 4.2 %all-to-all-start.2 = ((bf16[4,4,32,512]{3,2,1,0:T(8,128)(2,1)}), bf16[4,4,32,512]{3,2,1,0:T(8,128)(2,1)S(1)}, u32[]{:S(2)}, u32[]{:S(2)}) async-start(bf16[4,4,32,512]{3,2,1,0:T(8,128)(2,1)} %broadcast_in_dim.10), calls=%async_computation.2 | async-start | bytes 1048576 | tf_op jit(solution)/shard_map/all_to_all | solution.py:19
  90.6 3.9 %collective-permute-start.4 = (bf16[448,512]{1,0:T(8,128)(2,1)}, bf16[448,512]{1,0:T(8,128)(2,1)S(1)}, u32[]{:S(2)}, u32[]{:S(2)}) collective-permute-start(bf16[448,512]{1,0:T(8,128)(2,1)} %refs_0_), channel_id=1, source_target_pairs={{0,256},{256,512},{512,768},{768,0},{1,257},{257,513},{513,769},{7... | collective-permute-start | bytes 1376264 | tf_op jit(solution)/shard_map/ppermute | solution.py:31
  94.5 3.1 %collective-permute-start.5 = (bf16[448,512]{1,0:T(8,128)(2,1)}, bf16[448,512]{1,0:T(8,128)(2,1)}, u32[]{:S(2)}, u32[]{:S(2)}) collective-permute-start(bf16[448,512]{1,0:T(8,128)(2,1)} %refs_0_), channel_id=1, source_target_pairs={{0,768},{256,0},{512,256},{768,512},{1,769},{257,1},{513,257},{769... | collective-permute-start | bytes 1376264 | tf_op jit(solution)/shard_map/ppermute | solution.py:31
  97.7 4.7 %collective-permute-done.4.refs_1_ = bf16[448,512]{1,0:T(8,128)(2,1)S(1)} collective-permute-done((bf16[448,512]{1,0:T(8,128)(2,1)}, bf16[448,512]{1,0:T(8,128)(2,1)S(1)}, u32[]{:S(2)}, u32[]{:S(2)}) %collective-permute-start.4) | collective-permute-done | bytes 458784 | tf_op jit(solution)/shard_map/ppermute | solution.py:31
  102.4 0.0 copy-start.1
  102.4 0.8 copy-done.1
  103.2 2.1 collective-permute-done.5.refs_2_
  105.2 0.0 all-to-all-done.2.own_ref
  105.2 1.9 collective-permute-start.6
  107.2 1.9 collective-permute-done.6.other_ref
  109.0 0.0 copy-start.4
  109.0 1.0 copy-done.4
  110.1 2.3 %shard_map.55 = bf16[4,2,32,896]{3,2,1,0:T(8,128)(2,1)S(1)} custom-call(bf16[4,4,32,512]{3,2,1,0:T(8,128)(2,1)S(1)} %all-to-all-done.2.own_ref, bf16[4,4,32,512]{3,2,1,0:T(8,128)(2,1)S(1)} %collective-permute-done.6.other_ref, bf16[2,448,512]{2,1,0:T(8,128)(2,1)S(1)} %pad_maximum_fusion.refs_0_, bf16[2,448,512]{2,1,0:T(8,128)(2,1)S(1)} %collective-permute-done.refs_1_, ...), custom_call_target="tpu_custom_call" | custom-call | tf_op jit(solution)/shard_map/pallas_call | solution.py:59
  112.4 0.0 copy-start
  112.4 0.8 copy-done
  113.1 0.0 copy-start.2
  113.1 4.6 %all-to-all-start.3 = ((bf16[4,64,896]{2,1,0:T(8,128)(2,1)}), bf16[4,64,896]{2,1,0:T(8,128)(2,1)S(1)}, u32[]{:S(2)}, u32[]{:S(2)}) async-start(bf16[4,64,896]{2,1,0:T(8,128)(2,1)} %bitcast.20), calls=%async_computation.3 | async-start | bytes 917504 | tf_op jit(solution)/shard_map/all_to_all | solution.py:19
  117.7 0.0 copy-done.2
  117.7 2.6 %collective-permute-start.7 = (bf16[224,512]{1,0:T(8,128)(2,1)S(1)}, bf16[224,512]{1,0:T(8,128)(2,1)S(1)}, u32[]{:S(2)}, u32[]{:S(2)}) collective-permute-start(bf16[224,512]{1,0:T(8,128)(2,1)S(1)} %slice.20), channel_id=1, source_target_pairs={{0,256},{256,512},{512,768},{768,0},{1,257},{257,513},{513,769},{7... | collective-permute-start | bytes 688136 | tf_op jit(solution)/shard_map/ppermute | solution.py:31
  120.3 1.0 slice.21
  121.3 4.5 %collective-permute-start.8 = (bf16[224,512]{1,0:T(8,128)(2,1)S(1)}, bf16[224,512]{1,0:T(8,128)(2,1)S(1)}, u32[]{:S(2)}, u32[]{:S(2)}) collective-permute-start(bf16[224,512]{1,0:T(8,128)(2,1)S(1)} %slice.21), channel_id=1, source_target_pairs={{0,768},{256,0},{512,256},{768,512},{1,769},{257,1},{513,257},{769... | collective-permute-start | bytes 688136 | tf_op jit(solution)/shard_map/ppermute | solution.py:31
  125.8 2.4 %collective-permute-done.7.refs_3_ = bf16[224,512]{1,0:T(8,128)(2,1)S(1)} collective-permute-done((bf16[224,512]{1,0:T(8,128)(2,1)S(1)}, bf16[224,512]{1,0:T(8,128)(2,1)S(1)}, u32[]{:S(2)}, u32[]{:S(2)}) %collective-permute-start.7) | collective-permute-done | bytes 229408 | tf_op jit(solution)/shard_map/ppermute | solution.py:31
  128.2 2.1 %collective-permute-done.8.refs_4_ = bf16[224,512]{1,0:T(8,128)(2,1)S(1)} collective-permute-done((bf16[224,512]{1,0:T(8,128)(2,1)S(1)}, bf16[224,512]{1,0:T(8,128)(2,1)S(1)}, u32[]{:S(2)}, u32[]{:S(2)}) %collective-permute-start.8) | collective-permute-done | bytes 229408 | tf_op jit(solution)/shard_map/ppermute | solution.py:31
  130.4 0.0 all-to-all-done.3
  130.4 0.1 convert_reduce_fusion
  130.4 0.1 fusion
  130.5 0.0 copy-start.5
  130.6 11.1 %all_to_all.36.hidden_ref = bf16[4,64,448]{2,1,0:T(8,128)(2,1)S(1)} all-to-all(bf16[4,64,448]{2,1,0:T(8,128)(2,1)S(1)} %broadcast_in_dim.11), channel_id=1, replica_groups=mesh['x'=4,'y'=4,'zh'=8,'zl'=4,'c'=2] {'y'}, dimensions={0} | all-to-all | bytes 458752 | tf_op jit(solution)/shard_map/all_to_all | solution.py:19
  141.7 0.0 copy-done.5
  141.7 1.7 shard_map.56
  143.4 1.9 collective-permute-start.9
  145.4 1.9 collective-permute-done.9
  147.2 0.2 add_convert_fusion
  147.4 21.6 %all_to_all.37 = bf16[16,32,512]{2,1,0:T(8,128)(2,1)S(1)} all-to-all(bf16[16,32,512]{2,1,0:T(8,128)(2,1)S(1)} %bitcast.21), channel_id=1, replica_groups=mesh['x'=4,'y'=4,'zh'=8,'zl'=4,'c'=2] {'x','zl'}, dimensions={0} | all-to-all | bytes 1048576 | tf_op jit(solution)/shard_map/all_to_all | solution.py:19
  169.0 0.1 bitcast_reduce_fusion
  169.1 0.1 copy.12
  169.2 0.1 copy.13
  169.3 0.7 copy.14
  170.0 0.0 copy-start.7
  170.0 10.1 %all-to-all-start.6 = ((bf16[8,16,512]{2,1,0:T(8,128)(2,1)}), bf16[8,16,512]{2,1,0:T(8,128)(2,1)S(1)}, u32[]{:S(2)}, u32[]{:S(2)}) async-start(bf16[8,16,512]{2,1,0:T(8,128)(2,1)} %copy.14), calls=%async_computation.6 | async-start | bytes 262144 | tf_op jit(solution)/shard_map/all_to_all | solution.py:19
  180.0 0.0 copy-done.7
  180.1 30.2 %all-to-all-done.6 = bf16[8,16,512]{2,1,0:T(8,128)(2,1)S(1)} async-done(((bf16[8,16,512]{2,1,0:T(8,128)(2,1)}), bf16[8,16,512]{2,1,0:T(8,128)(2,1)S(1)}, u32[]{:S(2)}, u32[]{:S(2)}) %all-to-all-start.6) | async-done | bytes 131104 | tf_op jit(solution)/shard_map/all_to_all | solution.py:19
  210.2 0.7 multiply_convert_fusion
  (6 shorter events, 0.1 us)
Async XLA Ops:
  0.0 8.3 %copy-start.6 = (bf16[16,512]{1,0:T(8,128)(2,1)S(1)}, bf16[16,512]{1,0:T(8,128)(2,1)}, u32[]{:S(2)}) copy-start(bf16[16,512]{1,0:T(8,128)(2,1)} %param.5) | copy-start | bytes 49156
  1.3 54.5 %collective-permute-start = (bf16[2,448,512]{2,1,0:T(8,128)(2,1)S(1)}, bf16[2,448,512]{2,1,0:T(8,128)(2,1)S(1)}, u32[]{:S(2)}, u32[]{:S(2)}) collective-permute-start(bf16[2,448,512]{2,1,0:T(8,128)(2,1)S(1)} %pad_maximum_fusion.refs_0_), channel_id=1, source_target_pairs={{0,256},{256,512},{512,768},{768,0},{1,257},{257,513},{513,769},{7... | collective-permute-start | bytes 2752520 | tf_op jit(solution)/shard_map/ppermute | solution.py:31
  4.7 56.0 %collective-permute-start.2 = (bf16[2,448,512]{2,1,0:T(8,128)(2,1)S(1)}, bf16[2,448,512]{2,1,0:T(8,128)(2,1)S(1)}, u32[]{:S(2)}, u32[]{:S(2)}) collective-permute-start(bf16[2,448,512]{2,1,0:T(8,128)(2,1)S(1)} %pad_maximum_fusion.refs_0_), channel_id=1, source_target_pairs={{0,768},{256,0},{512,256},{768,512},{1,769},{257,1},{513,257},{769... | collective-permute-start | bytes 2752520 | tf_op jit(solution)/shard_map/ppermute | solution.py:31
  29.2 56.3 %all-to-all-start.1 = ((bf16[8,4,4,512]{3,2,1,0:T(4,128)(2,1)}), bf16[8,4,4,512]{3,2,1,0:T(4,128)(2,1)S(1)}, u32[]{:S(2)}, u32[]{:S(2)}) async-start(bf16[8,4,4,512]{3,2,1,0:T(4,128)(2,1)} %broadcast_in_dim.8), calls=%async_computation.1 | async-start | bytes 262144 | tf_op jit(solution)/shard_map/all_to_all | solution.py:19
  56.5 28.9 %collective-permute-start.1 = (bf16[448,512]{1,0:T(8,128)(2,1)}, bf16[448,512]{1,0:T(8,128)(2,1)S(1)}, u32[]{:S(2)}, u32[]{:S(2)}) collective-permute-start(bf16[448,512]{1,0:T(8,128)(2,1)} %slice_bitcast_fusion.1), channel_id=1, source_target_pairs={{0,256},{256,512},{512,768},{768,0},{1,257},{257,513},{513,769},{7... | collective-permute-start | bytes 1376264 | tf_op jit(solution)/shard_map/ppermute | solution.py:31
  61.5 24.0 %collective-permute-start.3 = (bf16[448,512]{1,0:T(8,128)(2,1)}, bf16[448,512]{1,0:T(8,128)(2,1)}, u32[]{:S(2)}, u32[]{:S(2)}) collective-permute-start(bf16[448,512]{1,0:T(8,128)(2,1)} %slice_bitcast_fusion), channel_id=1, source_target_pairs={{0,768},{256,0},{512,256},{768,512},{1,769},{257,1},{513,257},{769... | collective-permute-start | bytes 1376264 | tf_op jit(solution)/shard_map/ppermute | solution.py:31
  85.5 1.0 copy-start.3
  86.4 18.8 %all-to-all-start.2 = ((bf16[4,4,32,512]{3,2,1,0:T(8,128)(2,1)}), bf16[4,4,32,512]{3,2,1,0:T(8,128)(2,1)S(1)}, u32[]{:S(2)}, u32[]{:S(2)}) async-start(bf16[4,4,32,512]{3,2,1,0:T(8,128)(2,1)} %broadcast_in_dim.10), calls=%async_computation.2 | async-start | bytes 1048576 | tf_op jit(solution)/shard_map/all_to_all | solution.py:19
  90.6 11.8 %collective-permute-start.4 = (bf16[448,512]{1,0:T(8,128)(2,1)}, bf16[448,512]{1,0:T(8,128)(2,1)S(1)}, u32[]{:S(2)}, u32[]{:S(2)}) collective-permute-start(bf16[448,512]{1,0:T(8,128)(2,1)} %refs_0_), channel_id=1, source_target_pairs={{0,256},{256,512},{512,768},{768,0},{1,257},{257,513},{513,769},{7... | collective-permute-start | bytes 1376264 | tf_op jit(solution)/shard_map/ppermute | solution.py:31
  94.5 10.7 %collective-permute-start.5 = (bf16[448,512]{1,0:T(8,128)(2,1)}, bf16[448,512]{1,0:T(8,128)(2,1)}, u32[]{:S(2)}, u32[]{:S(2)}) collective-permute-start(bf16[448,512]{1,0:T(8,128)(2,1)} %refs_0_), channel_id=1, source_target_pairs={{0,768},{256,0},{512,256},{768,512},{1,769},{257,1},{513,257},{769... | collective-permute-start | bytes 1376264 | tf_op jit(solution)/shard_map/ppermute | solution.py:31
  102.4 0.8 copy-start.1
  105.2 3.8 %collective-permute-start.6 = (bf16[4,4,32,512]{3,2,1,0:T(8,128)(2,1)S(1)}, bf16[4,4,32,512]{3,2,1,0:T(8,128)(2,1)S(1)}, u32[]{:S(2)}, u32[]{:S(2)}) collective-permute-start(bf16[4,4,32,512]{3,2,1,0:T(8,128)(2,1)S(1)} %all-to-all-done.2.own_ref), channel_id=1, source_target_pairs={{0,1},{1,0},{2,3},{3,2},{4,5},{5,4},{6,7},{7,6},{8,9},{9,8},{10,11... | collective-permute-start | bytes 1572872 | tf_op jit(solution)/shard_map/ppermute | solution.py:27
  109.0 1.0 copy-start.4
  112.4 0.8 copy-start
  113.1 4.6 %copy-start.2 = (bf16[448,512]{1,0:T(8,128)(2,1)S(1)}, bf16[448,512]{1,0:T(8,128)(2,1)}, u32[]{:S(2)}) copy-start(bf16[448,512]{1,0:T(8,128)(2,1)} %copy-done.1) | copy-start | bytes 1376260
  113.1 17.2 %all-to-all-start.3 = ((bf16[4,64,896]{2,1,0:T(8,128)(2,1)}), bf16[4,64,896]{2,1,0:T(8,128)(2,1)S(1)}, u32[]{:S(2)}, u32[]{:S(2)}) async-start(bf16[4,64,896]{2,1,0:T(8,128)(2,1)} %bitcast.20), calls=%async_computation.3 | async-start | bytes 917504 | tf_op jit(solution)/shard_map/all_to_all | solution.py:19
  117.7 10.5 %collective-permute-start.7 = (bf16[224,512]{1,0:T(8,128)(2,1)S(1)}, bf16[224,512]{1,0:T(8,128)(2,1)S(1)}, u32[]{:S(2)}, u32[]{:S(2)}) collective-permute-start(bf16[224,512]{1,0:T(8,128)(2,1)S(1)} %slice.20), channel_id=1, source_target_pairs={{0,256},{256,512},{512,768},{768,0},{1,257},{257,513},{513,769},{7... | collective-permute-start | bytes 688136 | tf_op jit(solution)/shard_map/ppermute | solution.py:31
  121.3 9.1 %collective-permute-start.8 = (bf16[224,512]{1,0:T(8,128)(2,1)S(1)}, bf16[224,512]{1,0:T(8,128)(2,1)S(1)}, u32[]{:S(2)}, u32[]{:S(2)}) collective-permute-start(bf16[224,512]{1,0:T(8,128)(2,1)S(1)} %slice.21), channel_id=1, source_target_pairs={{0,768},{256,0},{512,256},{768,512},{1,769},{257,1},{513,257},{769... | collective-permute-start | bytes 688136 | tf_op jit(solution)/shard_map/ppermute | solution.py:31
  130.5 11.2 %copy-start.5 = (bf16[448,512]{1,0:T(8,128)(2,1)S(1)}, bf16[448,512]{1,0:T(8,128)(2,1)}, u32[]{:S(2)}) copy-start(bf16[448,512]{1,0:T(8,128)(2,1)} %refs_0_) | copy-start | bytes 1376260
  143.4 3.8 %collective-permute-start.9 = (bf16[4,128,512]{2,1,0:T(8,128)(2,1)S(1)}, bf16[4,128,512]{2,1,0:T(8,128)(2,1)S(1)}, u32[]{:S(2)}, u32[]{:S(2)}) collective-permute-start(bf16[4,128,512]{2,1,0:T(8,128)(2,1)S(1)} %get-tuple-element.28), channel_id=1, source_target_pairs={{0,1},{1,0},{2,3},{3,2},{4,5},{5,4},{6,7},{7,6},{8,9},{9,8},{10,11... | collective-permute-start | bytes 1572872 | tf_op jit(solution)/shard_map/ppermute | solution.py:27
  170.0 10.1 %copy-start.7 = (s32[16]{0:T(128)S(1)}, s32[16]{0:T(128)}, u32[]{:S(2)}) copy-start(s32[16]{0:T(128)} %param.6) | copy-start | bytes 196
  170.0 40.2 %all-to-all-start.6 = ((bf16[8,16,512]{2,1,0:T(8,128)(2,1)}), bf16[8,16,512]{2,1,0:T(8,128)(2,1)S(1)}, u32[]{:S(2)}, u32[]{:S(2)}) async-start(bf16[8,16,512]{2,1,0:T(8,128)(2,1)} %copy.14), calls=%async_computation.6 | async-start | bytes 262144 | tf_op jit(solution)/shard_map/all_to_all | solution.py:19

commit v4 on v1

v4 whole, which is shorter than its diff:
```python
import jax
import jax.numpy as jnp
from jax import lax
from jax.experimental import pallas as pl
from jax.experimental.pallas import tpu as pltpu
from jax.sharding import Mesh, PartitionSpec as P

XP, XL, Y, ZH, ZL, C = 2, 2, 4, 8, 4, 2
DP = ("zh", "zl", "c")
TENSOR = ("xp", "xl", "y")
F32 = jnp.float32
BF16 = jnp.bfloat16
VMEM = pl.BlockSpec(memory_space=pltpu.VMEM)
PARAMS = pltpu.CompilerParams(vmem_limit_bytes=24 << 20)


def exchange(pieces, axes):
    return lax.all_to_all(pieces, axes, split_axis=0, concat_axis=0, tiled=True)


def spread(block, count, axes):
    return exchange(jnp.broadcast_to(block[None], (count,) + block.shape), axes)


def swap(block, axis):
    return lax.ppermute(block, axis, [(0, 1), (1, 0)])


def first_kernel(tokens_ref, mine, beside, mine_other, beside_other, out_ref):
    feats = tokens_ref.shape[-1]
    place = lax.axis_index("xl")
    here = tokens_ref[place].reshape(-1, feats)
    there = tokens_ref[1 - place].reshape(-1, feats)
    columns = 2 * mine.shape[1]
    for core, (near, far) in enumerate(((mine, beside), (mine_other, beside_other))):
        total = None
        for block, weights in ((here, near), (there, far)):
            pair = weights[:2].reshape(columns, feats)
            term = lax.dot_general(block, pair, (((1,), (1,)), ((), ())), preferred_element_type=F32)
            total = term if total is None else total + term
        out_ref[:, core * columns : (core + 1) * columns] = total.astype(BF16)


def first(tokens, weights):
    rows = tokens.shape[1] * tokens.shape[2]
    return pl.pallas_call(
        first_kernel,
        out_shape=jax.ShapeDtypeStruct((rows, C * 2 * weights[0].shape[1]), BF16),
        in_specs=[VMEM] * (1 + len(weights)),
        out_specs=VMEM,
        compiler_params=PARAMS,
    )(tokens, *weights)


def activate_kernel(sums_ref, out_ref):
    width = out_ref.shape[3]
    sums = jnp.sum(sums_ref[...].astype(F32), axis=0)
    for core in range(C):
        pair = sums[:, core * 2 * width : (core + 1) * 2 * width]
        gate, up = pair[:, :width], pair[:, width:]
        hidden = (gate * jax.nn.sigmoid(gate) * up).astype(BF16)
        for copy in range(out_ref.shape[0]):
            out_ref[copy, core] = hidden


def activate(sums, copies):
    return pl.pallas_call(
        activate_kernel,
        out_shape=jax.ShapeDtypeStruct((copies, C, sums.shape[1], sums.shape[2] // (2 * C)), BF16),
        in_specs=[VMEM],
        out_specs=VMEM,
        compiler_params=PARAMS,
    )(sums)


def second_kernel(hidden_ref, mine, beside, mine_other, beside_other, out_ref):
    width = mine.shape[1]
    place = lax.axis_index("xl")
    hidden = [hidden_ref[:, core].reshape(-1, width) for core in range(C)]
    for block, weights in ((place, (mine, mine_other)), (1 - place, (beside, beside_other))):
        total = None
        for rows, downs in zip(hidden, weights):
            term = jnp.dot(rows, downs[2], preferred_element_type=F32)
            total = term if total is None else total + term
        out_ref[block] = total.astype(BF16)


def second(hidden, weights):
    return pl.pallas_call(
        second_kernel,
        out_shape=jax.ShapeDtypeStruct((XL, hidden.shape[0] * hidden.shape[2], weights[0].shape[2]), BF16),
        in_specs=[VMEM] * (1 + len(weights)),
        out_specs=VMEM,
        compiler_params=PARAMS,
    )(hidden, *weights)


def on_device(tokens, pad_mask, gate_weight, up_weight, down_weight):
    rows, feats = tokens.shape
    width = gate_weight.shape[1]
    sub = rows // XL
    some = ZH * sub

    mine = jnp.stack([gate_weight.T, up_weight.T, down_weight])
    beside = swap(mine, "xl")
    mine_other = swap(mine, "c")
    far = spread(tokens, ZH, "zh")
    far, beside, mine_other = lax.optimization_barrier((far, beside, mine_other))
    beside_other = swap(beside, "c")

    far = far.reshape(ZH, XL, sub, feats).transpose(1, 0, 2, 3).reshape(XL, 1, some, feats)
    far = jnp.broadcast_to(far, (XL, ZL, some, feats)).reshape(XL * ZL, some, feats)
    own = exchange(far, ("xl", "zl")).reshape(XL, ZL, some, feats)
    own, beside_other = lax.optimization_barrier((own, beside_other))
    weights = (mine, beside, mine_other, beside_other)

    groups = XP * Y
    few = ZL * some // groups
    sums = exchange(first(own, weights).reshape(groups, few, C * 2 * width), ("xp", "y"))
    hidden = exchange(activate(sums, groups), ("xp", "y"))

    part = second(hidden, weights).reshape(XL * ZL, some, feats)
    part = exchange(part, ("xl", "zl")).reshape(XL, ZL, some, feats)
    part = jnp.sum(part.astype(F32), axis=1).astype(BF16)
    part = part.reshape(XL, ZH, sub, feats).transpose(1, 0, 2, 3).reshape(ZH, rows, feats)
    result = jnp.sum(exchange(part, "zh").astype(F32), axis=0)
    return (result * pad_mask[:, None].astype(F32)).astype(BF16)


def solution(mesh):
    fine = Mesh(mesh.devices.reshape(XP, XL, Y, ZH, ZL, C), TENSOR + DP)
    placed = (P(DP, TENSOR), P(DP), P(TENSOR, DP), P(TENSOR, DP), P(DP, TENSOR))
    return jax.shard_map(
        on_device, mesh=fine, in_specs=placed, out_specs=P(DP, TENSOR), check_vma=False
    )
```

time: 243 us -> 173 us (0.71)
  the two profiles are of different devices: /device:TPU:8 before, /device:TPU:14 now
where the time goes in v4:
time: 173 us; the launch traced here: 172 us
  blocking collectives  104 us (60%)
  waiting for transfers between devices  36.4 us (21%)
  starting transfers between devices  20.9 us (12%)
  local copies, waits for them, and re-layouts  6.41 us (4%)
  other arithmetic  2.23 us (1%)
  Pallas kernels  2.12 us (1%)
    all_to_all x4, blocking collectives, exchange(): return lax.all_to_all(pieces, axes, split_axis=0, concat_axis=0, tiled=True)  104 us
    all_to_all x2, waiting for transfers between devices, exchange(): return lax.all_to_all(pieces, axes, split_axis=0, concat_axis=0, tiled=True)  33.3 us
    all_to_all x2, starting transfers between devices, exchange(): return lax.all_to_all(pieces, axes, split_axis=0, concat_axis=0, tiled=True)  14.3 us
    ppermute x3, starting transfers between devices, swap(): return lax.ppermute(block, axis, [(0, 1), (1, 0)])  6.57 us
    unnamed x16, local copies, waits for them, and re-layouts  4.89 us
  transfers between devices with their start and end apart: 5, of which 3 were waited for; matrix products, arithmetic and copies ran while one was open for 0% of the time, Pallas kernels for 0%

profile of v4, /device:TPU:14, one launch (start us, length us, event | category | flops | bytes accessed | tf_op | source)
XLA Modules:
  0.0 172.2 jit_solution(4107068145411183656)
XLA Ops:
  0.0 0.0 copy-start.6
  0.0 1.5 pad_maximum_fusion.mine
  1.5 2.7 %collective-permute-start = (bf16[3,448,512]{2,1,0:T(8,128)(2,1)S(1)}, bf16[3,448,512]{2,1,0:T(8,128)(2,1)S(1)}, u32[]{:S(2)}, u32[]{:S(2)}) collective-permute-start(bf16[3,448,512]{2,1,0:T(8,128)(2,1)S(1)} %pad_maximum_fusion.mine), channel_id=1, source_target_pairs={{0,256},{256,0},{1,257},{257,1},{2,258},{258,2},{3,259},{259,3},{4... | collective-permute-start | bytes 4128776 | tf_op jit(solution)/shard_map/ppermute | solution.py:26
  4.2 1.9 %collective-permute-start.1 = (bf16[3,448,512]{2,1,0:T(8,128)(2,1)S(1)}, bf16[3,448,512]{2,1,0:T(8,128)(2,1)S(1)}, u32[]{:S(2)}, u32[]{:S(2)}) collective-permute-start(bf16[3,448,512]{2,1,0:T(8,128)(2,1)S(1)} %pad_maximum_fusion.mine), channel_id=1, source_target_pairs={{0,1},{1,0},{2,3},{3,2},{4,5},{5,4},{6,7},{7,6},{8,9},{9,8},{10,11... | collective-permute-start | bytes 4128776 | tf_op jit(solution)/shard_map/ppermute | solution.py:26
  6.1 0.0 copy-done.6
  6.2 55.9 %all_to_all.30 = bf16[8,16,512]{2,1,0:T(8,128)(2,1)S(1)} all-to-all(bf16[8,16,512]{2,1,0:T(8,128)(2,1)S(1)} %broadcast_in_dim.6), channel_id=1, replica_groups=mesh['xp'=2,'xl'=2,'y'=4,'zh'=8,'zl'=4,'c'=2] {'zh'}, dimensions={0} | all-to-all | bytes 262144 | tf_op jit(solution)/shard_map/all_to_all | solution.py:18
  62.1 0.0 collective-permute-done.beside
  62.1 0.0 collective-permute-done.1.mine_other
  62.1 0.0 copy-start
  62.1 1.1 copy-done
  63.2 0.8 broadcast_in_dim.16
  64.1 8.0 %all-to-all-start.1 = ((bf16[8,64,512]{2,1,0:T(8,128)(2,1)}), bf16[8,64,512]{2,1,0:T(8,128)(2,1)S(1)}, u32[]{:S(2)}, u32[]{:S(2)}) async-start(bf16[8,64,512]{2,1,0:T(8,128)(2,1)} %bitcast.30), calls=%async_computation.1 | async-start | bytes 1048576 | tf_op jit(solution)/shard_map/all_to_all | solution.py:18
  72.1 1.9 %collective-permute-start.2 = (bf16[3,448,512]{2,1,0:T(8,128)(2,1)S(1)}, bf16[3,448,512]{2,1,0:T(8,128)(2,1)S(1)}, u32[]{:S(2)}, u32[]{:S(2)}) collective-permute-start(bf16[3,448,512]{2,1,0:T(8,128)(2,1)S(1)} %collective-permute-done.beside), channel_id=1, source_target_pairs={{0,1},{1,0},{2,3},{3,2},{4,5},{5,4},{6,7},{7,6},{8,9},{9,8},{10,11... | collective-permute-start | bytes 4128776 | tf_op jit(solution)/shard_map/ppermute | solution.py:26
  74.0 3.1 %collective-permute-done.2.beside_other = bf16[3,448,512]{2,1,0:T(8,128)(2,1)S(1)} collective-permute-done((bf16[3,448,512]{2,1,0:T(8,128)(2,1)S(1)}, bf16[3,448,512]{2,1,0:T(8,128)(2,1)S(1)}, u32[]{:S(2)}, u32[]{:S(2)}) %collective-permute-start.2) | collective-permute-done | bytes 1376288 | tf_op jit(solution)/shard_map/ppermute | solution.py:26
  77.1 0.0 copy-start.3
  77.1 1.1 copy-done.3
  78.2 5.8 %all-to-all-done.1 = bf16[8,64,512]{2,1,0:T(8,128)(2,1)S(1)} async-done(((bf16[8,64,512]{2,1,0:T(8,128)(2,1)}), bf16[8,64,512]{2,1,0:T(8,128)(2,1)S(1)}, u32[]{:S(2)}, u32[]{:S(2)}) %all-to-all-start.1) | async-done | bytes 524320 | tf_op jit(solution)/shard_map/all_to_all | solution.py:18
  84.1 0.0 copy-start.1
  84.1 1.3 copy-done.1
  85.4 0.0 copy-start.4
  85.4 1.3 copy-done.4
  86.7 1.3 shard_map.55
  88.0 0.0 copy-start.5
  88.0 16.0 %all_to_all.31.sums_ref = bf16[8,32,1792]{2,1,0:T(8,128)(2,1)S(1)} all-to-all(bf16[8,32,1792]{2,1,0:T(8,128)(2,1)S(1)} %bitcast.27), channel_id=1, replica_groups=mesh['xp'=2,'xl'=2,'y'=4,'zh'=8,'zl'=4,'c'=2] {'xp','y'}, dimensions={0} | all-to-all | bytes 1835008 | tf_op jit(solution)/shard_map/all_to_all | solution.py:18
  104.0 0.0 copy-start.2
  104.0 0.1 shard_map.56
  104.2 12.9 %all_to_all.32.hidden_ref = bf16[8,2,32,448]{3,2,1,0:T(8,128)(2,1)S(1)} all-to-all(bf16[8,2,32,448]{3,2,1,0:T(8,128)(2,1)S(1)} %shard_map.56), channel_id=1, replica_groups=mesh['xp'=2,'xl'=2,'y'=4,'zh'=8,'zl'=4,'c'=2] {'xp','y'}, dimensions={0} | all-to-all | bytes 917504 | tf_op jit(solution)/shard_map/all_to_all | solution.py:18
  117.0 0.0 copy-done.5
  117.0 0.0 copy-done.2
  117.0 0.7 shard_map.57
  117.7 0.0 copy-start.7
  117.8 19.2 %all_to_all.33 = bf16[8,64,512]{2,1,0:T(8,128)(2,1)S(1)} all-to-all(bf16[8,64,512]{2,1,0:T(8,128)(2,1)S(1)} %bitcast.28), channel_id=1, replica_groups=mesh['xp'=2,'xl'=2,'y'=4,'zh'=8,'zl'=4,'c'=2] {'xl','zl'}, dimensions={0} | all-to-all | bytes 1048576 | tf_op jit(solution)/shard_map/all_to_all | solution.py:18
  137.0 0.1 bitcast_reduce_fusion
  137.0 0.7 copy_bitcast_fusion
  137.7 6.3 %all-to-all-start.5 = ((bf16[8,16,512]{2,1,0:T(8,128)(2,1)}), bf16[8,16,512]{2,1,0:T(8,128)(2,1)S(1)}, u32[]{:S(2)}, u32[]{:S(2)}) async-start(bf16[8,16,512]{2,1,0:T(8,128)(2,1)} %copy_bitcast_fusion), calls=%async_computation.5 | async-start | bytes 262144 | tf_op jit(solution)/shard_map/all_to_all | solution.py:18
  144.0 0.0 copy-done.7
  144.0 27.5 %all-to-all-done.5 = bf16[8,16,512]{2,1,0:T(8,128)(2,1)S(1)} async-done(((bf16[8,16,512]{2,1,0:T(8,128)(2,1)}), bf16[8,16,512]{2,1,0:T(8,128)(2,1)S(1)}, u32[]{:S(2)}, u32[]{:S(2)}) %all-to-all-start.5) | async-done | bytes 131104 | tf_op jit(solution)/shard_map/all_to_all | solution.py:18
  171.5 0.7 multiply_convert_fusion
  (4 shorter events, 0.0 us)
Async XLA Ops:
  0.0 6.1 %copy-start.6 = (bf16[16,512]{1,0:T(8,128)(2,1)S(1)}, bf16[16,512]{1,0:T(8,128)(2,1)}, u32[]{:S(2)}) copy-start(bf16[16,512]{1,0:T(8,128)(2,1)} %param.5) | copy-start | bytes 49156
  1.5 60.6 %collective-permute-start = (bf16[3,448,512]{2,1,0:T(8,128)(2,1)S(1)}, bf16[3,448,512]{2,1,0:T(8,128)(2,1)S(1)}, u32[]{:S(2)}, u32[]{:S(2)}) collective-permute-start(bf16[3,448,512]{2,1,0:T(8,128)(2,1)S(1)} %pad_maximum_fusion.mine), channel_id=1, source_target_pairs={{0,256},{256,0},{1,257},{257,1},{2,258},{258,2},{3,259},{259,3},{4... | collective-permute-start | bytes 4128776 | tf_op jit(solution)/shard_map/ppermute | solution.py:26
  4.2 57.9 %collective-permute-start.1 = (bf16[3,448,512]{2,1,0:T(8,128)(2,1)S(1)}, bf16[3,448,512]{2,1,0:T(8,128)(2,1)S(1)}, u32[]{:S(2)}, u32[]{:S(2)}) collective-permute-start(bf16[3,448,512]{2,1,0:T(8,128)(2,1)S(1)} %pad_maximum_fusion.mine), channel_id=1, source_target_pairs={{0,1},{1,0},{2,3},{3,2},{4,5},{5,4},{6,7},{7,6},{8,9},{9,8},{10,11... | collective-permute-start | bytes 4128776 | tf_op jit(solution)/shard_map/ppermute | solution.py:26
  62.1 1.1 copy-start
  64.1 20.0 %all-to-all-start.1 = ((bf16[8,64,512]{2,1,0:T(8,128)(2,1)}), bf16[8,64,512]{2,1,0:T(8,128)(2,1)S(1)}, u32[]{:S(2)}, u32[]{:S(2)}) async-start(bf16[8,64,512]{2,1,0:T(8,128)(2,1)} %bitcast.30), calls=%async_computation.1 | async-start | bytes 1048576 | tf_op jit(solution)/shard_map/all_to_all | solution.py:18
  72.1 5.0 %collective-permute-start.2 = (bf16[3,448,512]{2,1,0:T(8,128)(2,1)S(1)}, bf16[3,448,512]{2,1,0:T(8,128)(2,1)S(1)}, u32[]{:S(2)}, u32[]{:S(2)}) collective-permute-start(bf16[3,448,512]{2,1,0:T(8,128)(2,1)S(1)} %collective-permute-done.beside), channel_id=1, source_target_pairs={{0,1},{1,0},{2,3},{3,2},{4,5},{5,4},{6,7},{7,6},{8,9},{9,8},{10,11... | collective-permute-start | bytes 4128776 | tf_op jit(solution)/shard_map/ppermute | solution.py:26
  77.1 1.1 copy-start.3
  84.1 1.3 copy-start.1
  85.4 1.3 copy-start.4
  88.0 29.0 %copy-start.5 = (bf16[3,448,512]{2,1,0:T(8,128)(2,1)S(1)}, bf16[3,448,512]{2,1,0:T(8,128)(2,1)}, u32[]{:S(2)}) copy-start(bf16[3,448,512]{2,1,0:T(8,128)(2,1)} %copy-done.3) | copy-start | bytes 4128772
  104.0 13.0 %copy-start.2 = (bf16[3,448,512]{2,1,0:T(8,128)(2,1)S(1)}, bf16[3,448,512]{2,1,0:T(8,128)(2,1)}, u32[]{:S(2)}) copy-start(bf16[3,448,512]{2,1,0:T(8,128)(2,1)} %copy-done) | copy-start | bytes 4128772
  117.7 26.2 %copy-start.7 = (s32[16]{0:T(128)S(1)}, s32[16]{0:T(128)}, u32[]{:S(2)}) copy-start(s32[16]{0:T(128)} %param.6) | copy-start | bytes 196
  137.7 33.8 %all-to-all-start.5 = ((bf16[8,16,512]{2,1,0:T(8,128)(2,1)}), bf16[8,16,512]{2,1,0:T(8,128)(2,1)S(1)}, u32[]{:S(2)}, u32[]{:S(2)}) async-start(bf16[8,16,512]{2,1,0:T(8,128)(2,1)} %copy_bitcast_fusion), calls=%async_computation.5 | async-start | bytes 262144 | tf_op jit(solution)/shard_map/all_to_all | solution.py:18

commit v5 on v4

--- a/solution.py
+++ b/solution.py
@@ -6,8 +6,14 @@
 from jax.sharding import Mesh, PartitionSpec as P
 
 XP, XL, Y, ZH, ZL, C = 2, 2, 4, 8, 4, 2
+Z = ZH * ZL
 DP = ("zh", "zl", "c")
 TENSOR = ("xp", "xl", "y")
+NEAR = [
+    [(xl * Z + (first * ZL + core * ZL // 2 + step) % Z) * C + core for xl in range(XL) for step in range(ZL)]
+    for core in range(C)
+    for first in range(ZH)
+]
 F32 = jnp.float32
 BF16 = jnp.bfloat16
 VMEM = pl.BlockSpec(memory_space=pltpu.VMEM)
@@ -18,6 +24,12 @@
     return lax.all_to_all(pieces, axes, split_axis=0, concat_axis=0, tiled=True)
 
 
+def near_exchange(pieces):
+    return lax.all_to_all(
+        pieces, ("xl",) + DP, split_axis=0, concat_axis=0, tiled=True, axis_index_groups=NEAR
+    )
+
+
 def spread(block, count, axes):
     return exchange(jnp.broadcast_to(block[None], (count,) + block.shape), axes)
 
@@ -26,8 +38,10 @@
     return lax.ppermute(block, axis, [(0, 1), (1, 0)])
 
 
-def first_kernel(tokens_ref, mine, beside, mine_other, beside_other, out_ref):
+def first_kernel(tokens_ref, mine, beside, mine_other, beside_other, out_ref, downs_ref):
     feats = tokens_ref.shape[-1]
+    for i, weights in enumerate((mine, beside, mine_other, beside_other)):
+        downs_ref[i] = weights[2]
     place = lax.axis_index("xl")
     here = tokens_ref[place].reshape(-1, feats)
     there = tokens_ref[1 - place].reshape(-1, feats)
@@ -45,9 +59,12 @@
     rows = tokens.shape[1] * tokens.shape[2]
     return pl.pallas_call(
         first_kernel,
-        out_shape=jax.ShapeDtypeStruct((rows, C * 2 * weights[0].shape[1]), BF16),
+        out_shape=(
+            jax.ShapeDtypeStruct((rows, C * 2 * weights[0].shape[1]), BF16),
+            jax.ShapeDtypeStruct((len(weights),) + weights[0].shape[1:], BF16),
+        ),
         in_specs=[VMEM] * (1 + len(weights)),
-        out_specs=VMEM,
+        out_specs=(VMEM, VMEM),
         compiler_params=PARAMS,
     )(tokens, *weights)
 
@@ -73,26 +90,26 @@
     )(sums)
 
 
-def second_kernel(hidden_ref, mine, beside, mine_other, beside_other, out_ref):
-    width = mine.shape[1]
+def second_kernel(hidden_ref, downs_ref, out_ref):
+    width = downs_ref.shape[1]
     place = lax.axis_index("xl")
     hidden = [hidden_ref[:, core].reshape(-1, width) for core in range(C)]
-    for block, weights in ((place, (mine, mine_other)), (1 - place, (beside, beside_other))):
+    for i, block in enumerate((place, 1 - place)):
         total = None
-        for rows, downs in zip(hidden, weights):
-            term = jnp.dot(rows, downs[2], preferred_element_type=F32)
+        for core, rows in enumerate(hidden):
+            term = jnp.dot(rows, downs_ref[C * core + i], preferred_element_type=F32)
             total = term if total is None else total + term
         out_ref[block] = total.astype(BF16)
 
 
-def second(hidden, weights):
+def second(hidden, downs):
     return pl.pallas_call(
         second_kernel,
-        out_shape=jax.ShapeDtypeStruct((XL, hidden.shape[0] * hidden.shape[2], weights[0].shape[2]), BF16),
-        in_specs=[VMEM] * (1 + len(weights)),
+        out_shape=jax.ShapeDtypeStruct((XL, hidden.shape[0] * hidden.shape[2], downs.shape[2]), BF16),
+        in_specs=[VMEM, VMEM],
         out_specs=VMEM,
         compiler_params=PARAMS,
-    )(hidden, *weights)
+    )(hidden, downs)
 
 
 def on_device(tokens, pad_mask, gate_weight, up_weight, down_weight):
@@ -103,24 +120,23 @@
 
     mine = jnp.stack([gate_weight.T, up_weight.T, down_weight])
     beside = swap(mine, "xl")
-    mine_other = swap(mine, "c")
     far = spread(tokens, ZH, "zh")
-    far, beside, mine_other = lax.optimization_barrier((far, beside, mine_other))
-    beside_other = swap(beside, "c")
+    far, beside, mine = lax.optimization_barrier((far, beside, mine))
+    mine_other, beside_other = swap(mine, "c"), swap(beside, "c")
 
     far = far.reshape(ZH, XL, sub, feats).transpose(1, 0, 2, 3).reshape(XL, 1, some, feats)
     far = jnp.broadcast_to(far, (XL, ZL, some, feats)).reshape(XL * ZL, some, feats)
-    own = exchange(far, ("xl", "zl")).reshape(XL, ZL, some, feats)
-    own, beside_other = lax.optimization_barrier((own, beside_other))
+    own = near_exchange(far).reshape(XL, ZL, some, feats)
     weights = (mine, beside, mine_other, beside_other)
 
     groups = XP * Y
     few = ZL * some // groups
-    sums = exchange(first(own, weights).reshape(groups, few, C * 2 * width), ("xp", "y"))
+    sums, downs = first(own, weights)
+    sums = exchange(sums.reshape(groups, few, C * 2 * width), ("xp", "y"))
     hidden = exchange(activate(sums, groups), ("xp", "y"))
 
-    part = second(hidden, weights).reshape(XL * ZL, some, feats)
-    part = exchange(part, ("xl", "zl")).reshape(XL, ZL, some, feats)
+    part = second(hidden, downs).reshape(XL * ZL, some, feats)
+    part = near_exchange(part).reshape(XL, ZL, some, feats)
     part = jnp.sum(part.astype(F32), axis=1).astype(BF16)
     part = part.reshape(XL, ZH, sub, feats).transpose(1, 0, 2, 3).reshape(ZH, rows, feats)
     result = jnp.sum(exchange(part, "zh").astype(F32), axis=0)

time: 173 us -> 169 us (0.977)
  the two profiles are of different devices: /device:TPU:14 before, /device:TPU:2 now
where the time goes in v5:
time: 169 us; the launch traced here: 168 us
  blocking collectives  95.5 us (57%)
  waiting for transfers between devices  32.1 us (19%)
  starting transfers between devices  29.6 us (18%)
  local copies, waits for them, and re-layouts  6.43 us (4%)
  other arithmetic  2.23 us (1%)
  Pallas kernels  2.15 us (1%)
    all_to_all x3, blocking collectives, exchange(): return lax.all_to_all(pieces, axes, split_axis=0, concat_axis=0, tiled=True)  76.4 us
    all_to_all x1, waiting for transfers between devices, exchange(): return lax.all_to_all(pieces, axes, split_axis=0, concat_axis=0, tiled=True)  28.2 us
    ppermute x3, starting transfers between devices, swap(): return lax.ppermute(block, axis, [(0, 1), (1, 0)])  19.6 us
    all_to_all x1, blocking collectives, near_exchange(): lax.all_to_all(pieces, ('xl',) + DP, split_axis=0, concat_axis=0, tiled=T...  19 us
    all_to_all x1, starting transfers between devices, near_exchange(): lax.all_to_all(pieces, ('xl',) + DP, split_axis=0, concat_axis=0, tiled=T...  6.27 us
    unnamed x12, local copies, waits for them, and re-layouts  4.89 us
    all_to_all x1, starting transfers between devices, exchange(): return lax.all_to_all(pieces, axes, split_axis=0, concat_axis=0, tiled=True)  3.67 us
  transfers between devices with their start and end apart: 5, of which 4 were waited for; matrix products, arithmetic and copies ran while one was open for 0% of the time, Pallas kernels for 0%

profile of v5, /device:TPU:2, one launch (start us, length us, event | category | flops | bytes accessed | tf_op | source)
XLA Modules:
  0.0 168.1 jit_solution(14810016540179061601)
XLA Ops:
  0.0 0.0 copy-start.4
  0.0 1.5 pad_maximum_fusion.mine
  1.5 15.1 %collective-permute-start = (bf16[3,448,512]{2,1,0:T(8,128)(2,1)S(1)}, bf16[3,448,512]{2,1,0:T(8,128)(2,1)S(1)}, u32[]{:S(2)}, u32[]{:S(2)}) collective-permute-start(bf16[3,448,512]{2,1,0:T(8,128)(2,1)S(1)} %pad_maximum_fusion.mine), channel_id=1, source_target_pairs={{0,256},{256,0},{1,257},{257,1},{2,258},{258,2},{3,259},{259,3},{4... | collective-permute-start | bytes 4128776 | tf_op jit(solution)/shard_map/ppermute | solution.py:38
  16.6 0.0 copy-done.4
  16.6 43.3 %all_to_all.30 = bf16[8,16,512]{2,1,0:T(8,128)(2,1)S(1)} all-to-all(bf16[8,16,512]{2,1,0:T(8,128)(2,1)S(1)} %broadcast_in_dim.6), channel_id=1, replica_groups=mesh['xp'=2,'xl'=2,'y'=4,'zh'=8,'zl'=4,'c'=2] {'zh'}, dimensions={0} | all-to-all | bytes 262144 | tf_op jit(solution)/shard_map/all_to_all | solution.py:24
  59.9 0.0 collective-permute-done.beside
  59.9 0.9 broadcast_in_dim.16
  60.7 6.3 %all-to-all-start.1 = ((bf16[8,64,512]{2,1,0:T(8,128)(2,1)}), bf16[8,64,512]{2,1,0:T(8,128)(2,1)S(1)}, u32[]{:S(2)}, u32[]{:S(2)}) async-start(bf16[8,64,512]{2,1,0:T(8,128)(2,1)} %bitcast.30), calls=%async_computation.1 | async-start | bytes 1048576 | tf_op jit(solution)/shard_map/all_to_all | solution.py:28
  67.0 2.6 %collective-permute-start.1 = (bf16[3,448,512]{2,1,0:T(8,128)(2,1)S(1)}, bf16[3,448,512]{2,1,0:T(8,128)(2,1)S(1)}, u32[]{:S(2)}, u32[]{:S(2)}) collective-permute-start(bf16[3,448,512]{2,1,0:T(8,128)(2,1)S(1)} %pad_maximum_fusion.mine), channel_id=1, source_target_pairs={{0,1},{1,0},{2,3},{3,2},{4,5},{5,4},{6,7},{7,6},{8,9},{9,8},{10,11... | collective-permute-start | bytes 4128776 | tf_op jit(solution)/shard_map/ppermute | solution.py:38
  69.6 1.9 %collective-permute-start.2 = (bf16[3,448,512]{2,1,0:T(8,128)(2,1)S(1)}, bf16[3,448,512]{2,1,0:T(8,128)(2,1)S(1)}, u32[]{:S(2)}, u32[]{:S(2)}) collective-permute-start(bf16[3,448,512]{2,1,0:T(8,128)(2,1)S(1)} %collective-permute-done.beside), channel_id=1, source_target_pairs={{0,1},{1,0},{2,3},{3,2},{4,5},{5,4},{6,7},{7,6},{8,9},{9,8},{10,11... | collective-permute-start | bytes 4128776 | tf_op jit(solution)/shard_map/ppermute | solution.py:38
  71.6 0.8 collective-permute-done.1.mine_other
  72.4 0.0 copy-start
  72.4 1.1 copy-done
  73.5 1.2 collective-permute-done.2.beside_other
  74.7 0.0 copy-start.2
  74.7 1.1 copy-done.2
  75.8 2.0 %all-to-all-done.1 = bf16[8,64,512]{2,1,0:T(8,128)(2,1)S(1)} async-done(((bf16[8,64,512]{2,1,0:T(8,128)(2,1)}), bf16[8,64,512]{2,1,0:T(8,128)(2,1)S(1)}, u32[]{:S(2)}, u32[]{:S(2)}) %all-to-all-start.1) | async-done | bytes 524320 | tf_op jit(solution)/shard_map/all_to_all | solution.py:28
  77.7 0.0 copy-start.1
  77.7 1.3 copy-done.1
  79.1 0.0 copy-start.3
  79.1 1.3 copy-done.3
  80.4 1.3 shard_map.55
  81.7 20.6 %all_to_all.31.sums_ref = bf16[8,32,1792]{2,1,0:T(8,128)(2,1)S(1)} all-to-all(bf16[8,32,1792]{2,1,0:T(8,128)(2,1)S(1)} %bitcast.29), channel_id=1, replica_groups=mesh['xp'=2,'xl'=2,'y'=4,'zh'=8,'zl'=4,'c'=2] {'xp','y'}, dimensions={0} | all-to-all | bytes 1835008 | tf_op jit(solution)/shard_map/all_to_all | solution.py:24
  102.3 0.1 shard_map.56
  102.4 12.6 %all_to_all.32.hidden_ref = bf16[8,2,32,448]{3,2,1,0:T(8,128)(2,1)S(1)} all-to-all(bf16[8,2,32,448]{3,2,1,0:T(8,128)(2,1)S(1)} %shard_map.56), channel_id=1, replica_groups=mesh['xp'=2,'xl'=2,'y'=4,'zh'=8,'zl'=4,'c'=2] {'xp','y'}, dimensions={0} | all-to-all | bytes 917504 | tf_op jit(solution)/shard_map/all_to_all | solution.py:24
  115.1 0.7 shard_map.57
  115.8 0.0 copy-start.5
  115.8 19.0 %all_to_all.33 = bf16[8,64,512]{2,1,0:T(8,128)(2,1)S(1)} all-to-all(bf16[8,64,512]{2,1,0:T(8,128)(2,1)S(1)} %bitcast.28), channel_id=1, replica_groups={{0,2,4,6,256,258,260,262},{8,10,12,14,264,266,268,270},{16,18,20,22,272..., dimensions={0} | all-to-all | bytes 1048576 | tf_op jit(solution)/shard_map/all_to_all | solution.py:28
  134.8 0.1 bitcast_reduce_fusion
  134.9 0.7 copy_bitcast_fusion
  135.5 3.7 %all-to-all-start.5 = ((bf16[8,16,512]{2,1,0:T(8,128)(2,1)}), bf16[8,16,512]{2,1,0:T(8,128)(2,1)S(1)}, u32[]{:S(2)}, u32[]{:S(2)}) async-start(bf16[8,16,512]{2,1,0:T(8,128)(2,1)} %copy_bitcast_fusion), calls=%async_computation.5 | async-start | bytes 262144 | tf_op jit(solution)/shard_map/all_to_all | solution.py:24
  139.2 0.0 copy-done.5
  139.2 28.2 %all-to-all-done.5 = bf16[8,16,512]{2,1,0:T(8,128)(2,1)S(1)} async-done(((bf16[8,16,512]{2,1,0:T(8,128)(2,1)}), bf16[8,16,512]{2,1,0:T(8,128)(2,1)S(1)}, u32[]{:S(2)}, u32[]{:S(2)}) %all-to-all-start.5) | async-done | bytes 131104 | tf_op jit(solution)/shard_map/all_to_all | solution.py:24
  167.4 0.7 multiply_convert_fusion
  (4 shorter events, 0.0 us)
Async XLA Ops:
  0.0 16.6 %copy-start.4 = (bf16[16,512]{1,0:T(8,128)(2,1)S(1)}, bf16[16,512]{1,0:T(8,128)(2,1)}, u32[]{:S(2)}) copy-start(bf16[16,512]{1,0:T(8,128)(2,1)} %param.5) | copy-start | bytes 49156
  1.5 58.4 %collective-permute-start = (bf16[3,448,512]{2,1,0:T(8,128)(2,1)S(1)}, bf16[3,448,512]{2,1,0:T(8,128)(2,1)S(1)}, u32[]{:S(2)}, u32[]{:S(2)}) collective-permute-start(bf16[3,448,512]{2,1,0:T(8,128)(2,1)S(1)} %pad_maximum_fusion.mine), channel_id=1, source_target_pairs={{0,256},{256,0},{1,257},{257,1},{2,258},{258,2},{3,259},{259,3},{4... | collective-permute-start | bytes 4128776 | tf_op jit(solution)/shard_map/ppermute | solution.py:38
  60.7 17.0 %all-to-all-start.1 = ((bf16[8,64,512]{2,1,0:T(8,128)(2,1)}), bf16[8,64,512]{2,1,0:T(8,128)(2,1)S(1)}, u32[]{:S(2)}, u32[]{:S(2)}) async-start(bf16[8,64,512]{2,1,0:T(8,128)(2,1)} %bitcast.30), calls=%async_computation.1 | async-start | bytes 1048576 | tf_op jit(solution)/shard_map/all_to_all | solution.py:28
  67.0 5.4 %collective-permute-start.1 = (bf16[3,448,512]{2,1,0:T(8,128)(2,1)S(1)}, bf16[3,448,512]{2,1,0:T(8,128)(2,1)S(1)}, u32[]{:S(2)}, u32[]{:S(2)}) collective-permute-start(bf16[3,448,512]{2,1,0:T(8,128)(2,1)S(1)} %pad_maximum_fusion.mine), channel_id=1, source_target_pairs={{0,1},{1,0},{2,3},{3,2},{4,5},{5,4},{6,7},{7,6},{8,9},{9,8},{10,11... | collective-permute-start | bytes 4128776 | tf_op jit(solution)/shard_map/ppermute | solution.py:38
  69.6 5.0 %collective-permute-start.2 = (bf16[3,448,512]{2,1,0:T(8,128)(2,1)S(1)}, bf16[3,448,512]{2,1,0:T(8,128)(2,1)S(1)}, u32[]{:S(2)}, u32[]{:S(2)}) collective-permute-start(bf16[3,448,512]{2,1,0:T(8,128)(2,1)S(1)} %collective-permute-done.beside), channel_id=1, source_target_pairs={{0,1},{1,0},{2,3},{3,2},{4,5},{5,4},{6,7},{7,6},{8,9},{9,8},{10,11... | collective-permute-start | bytes 4128776 | tf_op jit(solution)/shard_map/ppermute | solution.py:38
  72.4 1.1 copy-start
  74.7 1.1 copy-start.2
  77.7 1.3 copy-start.1
  79.1 1.3 copy-start.3
  115.8 23.5 %copy-start.5 = (s32[16]{0:T(128)S(1)}, s32[16]{0:T(128)}, u32[]{:S(2)}) copy-start(s32[16]{0:T(128)} %param.6) | copy-start | bytes 196
  135.5 31.8 %all-to-all-start.5 = ((bf16[8,16,512]{2,1,0:T(8,128)(2,1)}), bf16[8,16,512]{2,1,0:T(8,128)(2,1)S(1)}, u32[]{:S(2)}, u32[]{:S(2)}) async-start(bf16[8,16,512]{2,1,0:T(8,128)(2,1)} %copy_bitcast_fusion), calls=%async_computation.5 | async-start | bytes 262144 | tf_op jit(solution)/shard_map/all_to_all | solution.py:24

commit v6 on v5

v6 whole, which is shorter than its diff:
```python
import jax
import jax.numpy as jnp
from jax import lax
from jax.experimental import pallas as pl
from jax.experimental.pallas import tpu as pltpu
from jax.sharding import Mesh, PartitionSpec as P

XP, XL, Y, ZH, ZL, C = 2, 2, 4, 8, 4, 2
Z = ZH * ZL
DP = ("zh", "zl", "c")
TENSOR = ("xp", "xl", "y")
NEAR = [
    [(xl * Z + (first * ZL + core * ZL // 2 + step) % Z) * C + core for xl in range(XL) for step in range(ZL)]
    for core in range(C)
    for first in range(ZH)
]
F32 = jnp.float32
BF16 = jnp.bfloat16
VMEM = pl.BlockSpec(memory_space=pltpu.VMEM)
PARAMS = pltpu.CompilerParams(vmem_limit_bytes=24 << 20)


def exchange(pieces, axes):
    return lax.all_to_all(pieces, axes, split_axis=0, concat_axis=0, tiled=True)


def near_exchange(pieces):
    return lax.all_to_all(
        pieces, ("xl",) + DP, split_axis=0, concat_axis=0, tiled=True, axis_index_groups=NEAR
    )


def spread(block, count, axes):
    return exchange(jnp.broadcast_to(block[None], (count,) + block.shape), axes)


def swap(block, axis):
    return lax.ppermute(block, axis, [(0, 1), (1, 0)])


def first_kernel(tokens_ref, *refs):
    weights, out_ref = refs[:-1], refs[-1]
    feats = tokens_ref.shape[-1]
    place = lax.axis_index("xl")
    blocks = [tokens_ref[block].reshape(-1, feats) for block in (place, 1 - place)]
    columns = out_ref.shape[1] // C
    for core in range(C):
        total = None
        for step, block in enumerate(blocks):
            gate_up = weights[4 * core + 2 * step : 4 * core + 2 * step + 2]
            pair = jnp.concatenate([ref[...] for ref in gate_up], axis=0)
            term = lax.dot_general(block, pair, (((1,), (1,)), ((), ())), preferred_element_type=F32)
            total = term if total is None else total + term
        out_ref[:, core * columns : (core + 1) * columns] = total.astype(BF16)


def first(tokens, weights):
    rows = tokens.shape[1] * tokens.shape[2]
    return pl.pallas_call(
        first_kernel,
        out_shape=jax.ShapeDtypeStruct((rows, C * 2 * weights[0].shape[0]), BF16),
        in_specs=[VMEM] * (1 + len(weights)),
        out_specs=VMEM,
        compiler_params=PARAMS,
    )(tokens, *weights)


def activate_kernel(sums_ref, out_ref):
    width = out_ref.shape[3]
    sums = jnp.sum(sums_ref[...].astype(F32), axis=0)
    for core in range(C):
        pair = sums[:, core * 2 * width : (core + 1) * 2 * width]
        gate, up = pair[:, :width], pair[:, width:]
        hidden = (gate * jax.nn.sigmoid(gate) * up).astype(BF16)
        for copy in range(out_ref.shape[0]):
            out_ref[copy, core] = hidden


def activate(sums, copies):
    return pl.pallas_call(
        activate_kernel,
        out_shape=jax.ShapeDtypeStruct((copies, C, sums.shape[1], sums.shape[2] // (2 * C)), BF16),
        in_specs=[VMEM],
        out_specs=VMEM,
        compiler_params=PARAMS,
    )(sums)


def second_kernel(hidden_ref, *refs):
    weights, out_ref = refs[:-1], refs[-1]
    place = lax.axis_index("xl")
    hidden = [hidden_ref[:, core].reshape(-1, hidden_ref.shape[3]) for core in range(C)]
    for step, block in enumerate((place, 1 - place)):
        total = None
        for core, rows in enumerate(hidden):
            term = jnp.dot(rows, weights[C * core + step][...], preferred_element_type=F32)
            total = term if total is None else total + term
        out_ref[block] = total.astype(BF16)


def second(hidden, weights):
    rows = hidden.shape[0] * hidden.shape[2]
    return pl.pallas_call(
        second_kernel,
        out_shape=jax.ShapeDtypeStruct((XL, rows, weights[0].shape[1]), BF16),
        in_specs=[VMEM] * (1 + len(weights)),
        out_specs=VMEM,
        compiler_params=PARAMS,
    )(hidden, *weights)


def near_sum_kernel(parts_ref, out_ref):
    feats = parts_ref.shape[2]
    sums = []
    for xl in range(XL):
        total = jnp.sum(parts_ref[xl * ZL : (xl + 1) * ZL].astype(F32), axis=0)
        sums.append(total.reshape(ZH, -1, feats))
    out_ref[...] = jnp.concatenate(sums, axis=1).astype(BF16)


def near_sum(parts):
    return pl.pallas_call(
        near_sum_kernel,
        out_shape=jax.ShapeDtypeStruct((ZH, XL * parts.shape[1] // ZH, parts.shape[2]), BF16),
        in_specs=[VMEM],
        out_specs=VMEM,
        compiler_params=PARAMS,
    )(parts)


def far_sum_kernel(parts_ref, mask_ref, out_ref):
    total = jnp.sum(parts_ref[...].astype(F32), axis=0)
    out_ref[...] = (total * mask_ref[...].astype(F32)).astype(BF16)


def far_sum(parts, mask):
    return pl.pallas_call(
        far_sum_kernel,
        out_shape=jax.ShapeDtypeStruct(parts.shape[1:], BF16),
        in_specs=[VMEM, VMEM],
        out_specs=VMEM,
        compiler_params=PARAMS,
    )(parts, mask)


def on_device(tokens, pad_mask, gate_weight, up_weight, down_weight):
    rows, feats = tokens.shape
    width = gate_weight.shape[1]
    sub = rows // XL
    some = ZH * sub

    far = spread(tokens, ZH, "zh")
    mine = (gate_weight.T, up_weight.T, down_weight)
    beside = tuple(swap(block, "xl") for block in mine)
    mine_other = tuple(swap(block, "c") for block in mine[:2])
    far, beside, mine_other, down = lax.optimization_barrier((far, beside, mine_other, mine[2]))
    mine_other += (swap(down, "c"),)
    beside_other = tuple(swap(block, "c") for block in beside)
    weights = (mine, beside, mine_other, beside_other)
    gate_ups = [block for blocks in weights for block in blocks[:2]]
    downs = [blocks[2] for blocks in weights]

    far = far.reshape(ZH, XL, sub, feats).transpose(1, 0, 2, 3).reshape(XL, 1, some, feats)
    far = jnp.broadcast_to(far, (XL, ZL, some, feats)).reshape(XL * ZL, some, feats)
    own = near_exchange(far).reshape(XL, ZL, some, feats)

    groups = XP * Y
    few = ZL * some // groups
    sums = first(own, gate_ups)
    sums = exchange(sums.reshape(groups, few, C * 2 * width), ("xp", "y"))
    hidden = exchange(activate(sums, groups), ("xp", "y"))

    part = near_exchange(second(hidden, downs).reshape(XL * ZL, some, feats))
    part = exchange(near_sum(part), "zh")
    return far_sum(part, pad_mask[:, None])


def solution(mesh):
    fine = Mesh(mesh.devices.reshape(XP, XL, Y, ZH, ZL, C), TENSOR + DP)
    placed = (P(DP, TENSOR), P(DP), P(TENSOR, DP), P(TENSOR, DP), P(DP, TENSOR))
    return jax.shard_map(
        on_device, mesh=fine, in_specs=placed, out_specs=P(DP, TENSOR), check_vma=False
    )
```

time: 169 us -> 188 us (1.11)
  the two profiles are of different devices: /device:TPU:2 before, /device:TPU:32 now
where the time goes in v6:
time: 188 us; the launch traced here: 187 us
  starting transfers between devices  84.5 us (45%)
  waiting for transfers between devices  72.2 us (38%)
  blocking collectives  17.4 us (9%)
  local copies, waits for them, and re-layouts  6.58 us (4%)
  Pallas kernels  6.32 us (3%)
    all_to_all x4, starting transfers between devices, exchange(): return lax.all_to_all(pieces, axes, split_axis=0, concat_axis=0, tiled=True)  56.3 us
    all_to_all x4, waiting for transfers between devices, exchange(): return lax.all_to_all(pieces, axes, split_axis=0, concat_axis=0, tiled=True)  47.7 us
    ppermute x9, starting transfers between devices, swap(): return lax.ppermute(block, axis, [(0, 1), (1, 0)])  23 us
    ppermute x9, waiting for transfers between devices, swap(): return lax.ppermute(block, axis, [(0, 1), (1, 0)])  21.5 us
    all_to_all x1, blocking collectives, near_exchange(): lax.all_to_all(pieces, ('xl',) + DP, split_axis=0, concat_axis=0, tiled=T...  17.4 us
    all_to_all x1, starting transfers between devices, near_exchange(): lax.all_to_all(pieces, ('xl',) + DP, split_axis=0, concat_axis=0, tiled=T...  5.27 us
    unnamed x16, local copies, waits for them, and re-layouts  4.26 us
  transfers between devices with their start and end apart: 14, of which 8 were waited for; matrix products, arithmetic and copies ran while one was open for 0% of the time, Pallas kernels for 1%

profile of v6, /device:TPU:32, one launch (start us, length us, event | category | flops | bytes accessed | tf_op | source)
XLA Modules:
  0.0 187.1 jit_solution(7086935666080186591)
XLA Ops:
  0.0 1.4 broadcast_in_dim.16
  1.4 27.4 %all-to-all-start = ((bf16[8,16,512]{2,1,0:T(8,128)(2,1)}), bf16[8,16,512]{2,1,0:T(8,128)(2,1)S(1)}, u32[]{:S(2)}, u32[]{:S(2)}) async-start(bf16[8,16,512]{2,1,0:T(8,128)(2,1)} %broadcast_in_dim.16), calls=%async_computation | async-start | bytes 262144 | tf_op jit(solution)/shard_map/all_to_all | solution.py:24
  28.8 3.4 %collective-permute-start = (bf16[448,512]{1,0:T(8,128)(2,1)}, bf16[448,512]{1,0:T(8,128)(2,1)S(1)}, u32[]{:S(2)}, u32[]{:S(2)}) collective-permute-start(bf16[448,512]{1,0:T(8,128)(2,1)} %bitcast.16), channel_id=1, source_target_pairs={{0,256},{256,0},{1,257},{257,1},{2,258},{258,2},{3,259},{259,3},{4... | collective-permute-start | bytes 1376264 | tf_op jit(solution)/shard_map/ppermute | solution.py:38
  32.2 1.9 %collective-permute-start.3 = (bf16[448,512]{1,0:T(8,128)(2,1)}, bf16[448,512]{1,0:T(8,128)(2,1)S(1)}, u32[]{:S(2)}, u32[]{:S(2)}) collective-permute-start(bf16[448,512]{1,0:T(8,128)(2,1)} %bitcast.17), channel_id=1, source_target_pairs={{0,1},{1,0},{2,3},{3,2},{4,5},{5,4},{6,7},{7,6},{8,9},{9,8},{10,11... | collective-permute-start | bytes 1376264 | tf_op jit(solution)/shard_map/ppermute | solution.py:38
  34.2 2.4 %collective-permute-start.1 = (bf16[448,512]{1,0:T(8,128)(2,1)}, bf16[448,512]{1,0:T(8,128)(2,1)S(1)}, u32[]{:S(2)}, u32[]{:S(2)}) collective-permute-start(bf16[448,512]{1,0:T(8,128)(2,1)} %bitcast.19), channel_id=1, source_target_pairs={{0,256},{256,0},{1,257},{257,1},{2,258},{258,2},{3,259},{259,3},{4... | collective-permute-start | bytes 1376264 | tf_op jit(solution)/shard_map/ppermute | solution.py:38
  36.6 2.1 %collective-permute-start.4 = (bf16[448,512]{1,0:T(8,128)(2,1)}, bf16[448,512]{1,0:T(8,128)(2,1)S(1)}, u32[]{:S(2)}, u32[]{:S(2)}) collective-permute-start(bf16[448,512]{1,0:T(8,128)(2,1)} %bitcast.20), channel_id=1, source_target_pairs={{0,1},{1,0},{2,3},{3,2},{4,5},{5,4},{6,7},{7,6},{8,9},{9,8},{10,11... | collective-permute-start | bytes 1376264 | tf_op jit(solution)/shard_map/ppermute | solution.py:38
  38.7 3.4 %collective-permute-start.2 = (bf16[448,512]{1,0:T(8,128)(2,1)}, bf16[448,512]{1,0:T(8,128)(2,1)}, u32[]{:S(2)}, u32[]{:S(2)}) collective-permute-start(bf16[448,512]{1,0:T(8,128)(2,1)} %refs_0_.1), channel_id=1, source_target_pairs={{0,256},{256,0},{1,257},{257,1},{2,258},{258,2},{3,259},{259,3},{4... | collective-permute-start | bytes 1376264 | tf_op jit(solution)/shard_map/ppermute | solution.py:38
  42.2 2.2 %collective-permute-done.refs_2_ = bf16[448,512]{1,0:T(8,128)(2,1)S(1)} collective-permute-done((bf16[448,512]{1,0:T(8,128)(2,1)}, bf16[448,512]{1,0:T(8,128)(2,1)S(1)}, u32[]{:S(2)}, u32[]{:S(2)}) %collective-permute-start) | collective-permute-done | bytes 458784 | tf_op jit(solution)/shard_map/ppermute | solution.py:38
  44.4 9.8 %collective-permute-done.1.refs_3_ = bf16[448,512]{1,0:T(8,128)(2,1)S(1)} collective-permute-done((bf16[448,512]{1,0:T(8,128)(2,1)}, bf16[448,512]{1,0:T(8,128)(2,1)S(1)}, u32[]{:S(2)}, u32[]{:S(2)}) %collective-permute-start.1) | collective-permute-done | bytes 458784 | tf_op jit(solution)/shard_map/ppermute | solution.py:38
  54.2 0.0 collective-permute-done.3.refs_4_
  54.2 0.0 collective-permute-done.4.refs_5_
  54.2 8.5 %collective-permute-done.2.refs_1_ = bf16[448,512]{1,0:T(8,128)(2,1)} collective-permute-done((bf16[448,512]{1,0:T(8,128)(2,1)}, bf16[448,512]{1,0:T(8,128)(2,1)}, u32[]{:S(2)}, u32[]{:S(2)}) %collective-permute-start.2) | collective-permute-done | bytes 458784 | tf_op jit(solution)/shard_map/ppermute | solution.py:38
  62.7 0.0 all-to-all-done
  62.7 0.8 broadcast_in_dim.18
  63.5 0.0 copy-start
  63.5 0.0 copy-start.1
  63.5 5.3 %all-to-all-start.1 = ((bf16[8,64,512]{2,1,0:T(8,128)(2,1)}), bf16[8,64,512]{2,1,0:T(8,128)(2,1)S(1)}, u32[]{:S(2)}, u32[]{:S(2)}) async-start(bf16[8,64,512]{2,1,0:T(8,128)(2,1)} %bitcast.22), calls=%async_computation.1 | async-start | bytes 1048576 | tf_op jit(solution)/shard_map/all_to_all | solution.py:28
  68.8 3.4 %collective-permute-start.5 = (bf16[448,512]{1,0:T(8,128)(2,1)S(1)}, bf16[448,512]{1,0:T(8,128)(2,1)S(1)}, u32[]{:S(2)}, u32[]{:S(2)}) collective-permute-start(bf16[448,512]{1,0:T(8,128)(2,1)S(1)} %collective-permute-done.refs_2_), channel_id=1, source_target_pairs={{0,1},{1,0},{2,3},{3,2},{4,5},{5,4},{6,7},{7,6},{8,9},{9,8},{10,11... | collective-permute-start | bytes 1376264 | tf_op jit(solution)/shard_map/ppermute | solution.py:38
  72.2 1.9 %collective-permute-start.6 = (bf16[448,512]{1,0:T(8,128)(2,1)S(1)}, bf16[448,512]{1,0:T(8,128)(2,1)S(1)}, u32[]{:S(2)}, u32[]{:S(2)}) collective-permute-start(bf16[448,512]{1,0:T(8,128)(2,1)S(1)} %collective-permute-done.1.refs_3_), channel_id=1, source_target_pairs={{0,1},{1,0},{2,3},{3,2},{4,5},{5,4},{6,7},{7,6},{8,9},{9,8},{10,11... | collective-permute-start | bytes 1376264 | tf_op jit(solution)/shard_map/ppermute | solution.py:38
  74.2 0.0 collective-permute-done.5.refs_6_
  74.2 0.0 copy-start.2
  74.2 0.8 copy-done.2
  75.0 1.0 collective-permute-done.6.refs_7_
  76.0 0.0 copy-start.4
  76.0 0.8 copy-done.4
  76.7 3.0 %all-to-all-done.1 = bf16[8,64,512]{2,1,0:T(8,128)(2,1)S(1)} async-done(((bf16[8,64,512]{2,1,0:T(8,128)(2,1)}), bf16[8,64,512]{2,1,0:T(8,128)(2,1)S(1)}, u32[]{:S(2)}, u32[]{:S(2)}) %all-to-all-start.1) | async-done | bytes 524320 | tf_op jit(solution)/shard_map/all_to_all | solution.py:28
  79.7 0.0 copy-done
  79.7 0.0 copy-done.1
  79.7 0.0 copy-start.3
  79.7 1.0 copy-done.3
  80.8 0.0 copy-start.5
  80.8 1.0 copy-done.5
  81.8 2.3 %shard_map.55 = bf16[256,1792]{1,0:T(8,128)(2,1)} custom-call(bf16[2,4,64,512]{3,2,1,0:T(8,128)(2,1)S(1)} %bitcast.14, bf16[448,512]{1,0:T(8,128)(2,1)S(1)} %bitcast.18, bf16[448,512]{1,0:T(8,128)(2,1)S(1)} %bitcast.21, bf16[448,512]{1,0:T(8,128)(2,1)S(1)} %collective-permute-done.refs_2_, bf16[448,512]{1,0:T(8,128)(2,1)S(1)} %collective-permute-done.1.refs_3_, ...), custom_call_target="tpu_custom_call" | custom-call | tf_op jit(solution)/shard_map/pallas_call | solution.py:59
  84.0 0.0 copy-start.6
  84.0 6.8 %all-to-all-start.2 = ((bf16[8,32,1792]{2,1,0:T(8,128)(2,1)}), bf16[8,32,1792]{2,1,0:T(8,128)(2,1)S(1)}, u32[]{:S(2)}, u32[]{:S(2)}) async-start(bf16[8,32,1792]{2,1,0:T(8,128)(2,1)} %bitcast.7), calls=%async_computation.2 | async-start | bytes 1835008 | tf_op jit(solution)/shard_map/all_to_all | solution.py:24
  90.8 1.9 %collective-permute-start.8 = (bf16[448,512]{1,0:T(8,128)(2,1)}, bf16[448,512]{1,0:T(8,128)(2,1)S(1)}, u32[]{:S(2)}, u32[]{:S(2)}) collective-permute-start(bf16[448,512]{1,0:T(8,128)(2,1)} %collective-permute-done.2.refs_1_), channel_id=1, source_target_pairs={{0,1},{1,0},{2,3},{3,2},{4,5},{5,4},{6,7},{7,6},{8,9},{9,8},{10,11... | collective-permute-start | bytes 1376264 | tf_op jit(solution)/shard_map/ppermute | solution.py:38
  92.7 0.0 copy-done.6
  92.7 2.4 %collective-permute-start.7 = (bf16[448,512]{1,0:T(8,128)(2,1)S(1)}, bf16[448,512]{1,0:T(8,128)(2,1)S(1)}, u32[]{:S(2)}, u32[]{:S(2)}) collective-permute-start(bf16[448,512]{1,0:T(8,128)(2,1)S(1)} %copy-done.6), channel_id=1, source_target_pairs={{0,1},{1,0},{2,3},{3,2},{4,5},{5,4},{6,7},{7,6},{8,9},{9,8},{10,11... | collective-permute-start | bytes 1376264 | tf_op jit(solution)/shard_map/ppermute | solution.py:38
  95.1 8.9 %all-to-all-done.2.sums_ref = bf16[8,32,1792]{2,1,0:T(8,128)(2,1)S(1)} async-done(((bf16[8,32,1792]{2,1,0:T(8,128)(2,1)}), bf16[8,32,1792]{2,1,0:T(8,128)(2,1)S(1)}, u32[]{:S(2)}, u32[]{:S(2)}) %all-to-all-start.2) | async-done | bytes 917536 | tf_op jit(solution)/shard_map/all_to_all | solution.py:24
  104.0 0.9 shard_map.56
  105.0 3.7 %all-to-all-start.3 = ((bf16[8,2,32,448]{3,2,1,0:T(8,128)(2,1)}), bf16[8,2,32,448]{3,2,1,0:T(8,128)(2,1)S(1)}, u32[]{:S(2)}, u32[]{:S(2)}) async-start(bf16[8,2,32,448]{3,2,1,0:T(8,128)(2,1)} %shard_map.56), calls=%async_computation.3 | async-start | bytes 1048576 | tf_op jit(solution)/shard_map/all_to_all | solution.py:24
  108.6 0.0 collective-permute-done.8.refs_3_
  108.6 0.0 collective-permute-done.7.refs_2_
  108.6 10.8 %all-to-all-done.3.hidden_ref = bf16[8,2,32,448]{3,2,1,0:T(8,128)(2,1)S(1)} async-done(((bf16[8,2,32,448]{3,2,1,0:T(8,128)(2,1)}), bf16[8,2,32,448]{3,2,1,0:T(8,128)(2,1)S(1)}, u32[]{:S(2)}, u32[]{:S(2)}) %all-to-all-start.3) | async-done | bytes 458784 | tf_op jit(solution)/shard_map/all_to_all | solution.py:24
  119.4 1.7 shard_map.57
  121.1 17.4 %all_to_all.30.parts_ref = bf16[8,64,512]{2,1,0:T(8,128)(2,1)S(1)} all-to-all(bf16[8,64,512]{2,1,0:T(8,128)(2,1)S(1)} %bitcast.15), channel_id=1, replica_groups={{0,2,4,6,256,258,260,262},{8,10,12,14,264,266,268,270},{16,18,20,22,272..., dimensions={0} | all-to-all | bytes 1048576 | tf_op jit(solution)/shard_map/all_to_all | solution.py:28
  138.5 0.7 shard_map.58
  139.2 18.4 %all-to-all-start.5 = ((bf16[8,16,512]{2,1,0:T(8,128)(2,1)}), bf16[8,16,512]{2,1,0:T(8,128)(2,1)S(1)}, u32[]{:S(2)}, u32[]{:S(2)}) async-start(bf16[8,16,512]{2,1,0:T(8,128)(2,1)} %shard_map.58), calls=%async_computation.5 | async-start | bytes 262144 | tf_op jit(solution)/shard_map/all_to_all | solution.py:24
  157.6 0.0 copy-start.7
  157.6 0.7 copy-done.7
  158.3 0.1 copy.9.mask_ref
  158.3 28.1 %all-to-all-done.5.parts_ref = bf16[8,16,512]{2,1,0:T(8,128)(2,1)S(1)} async-done(((bf16[8,16,512]{2,1,0:T(8,128)(2,1)}), bf16[8,16,512]{2,1,0:T(8,128)(2,1)S(1)}, u32[]{:S(2)}, u32[]{:S(2)}) %all-to-all-start.5) | async-done | bytes 131104 | tf_op jit(solution)/shard_map/all_to_all | solution.py:24
  186.4 0.7 shard_map.59
  (1 shorter events, 0.0 us)
Async XLA Ops:
  1.4 61.3 %all-to-all-start = ((bf16[8,16,512]{2,1,0:T(8,128)(2,1)}), bf16[8,16,512]{2,1,0:T(8,128)(2,1)S(1)}, u32[]{:S(2)}, u32[]{:S(2)}) async-start(bf16[8,16,512]{2,1,0:T(8,128)(2,1)} %broadcast_in_dim.16), calls=%async_computation | async-start | bytes 262144 | tf_op jit(solution)/shard_map/all_to_all | solution.py:24
  28.8 15.5 %collective-permute-start = (bf16[448,512]{1,0:T(8,128)(2,1)}, bf16[448,512]{1,0:T(8,128)(2,1)S(1)}, u32[]{:S(2)}, u32[]{:S(2)}) collective-permute-start(bf16[448,512]{1,0:T(8,128)(2,1)} %bitcast.16), channel_id=1, source_target_pairs={{0,256},{256,0},{1,257},{257,1},{2,258},{258,2},{3,259},{259,3},{4... | collective-permute-start | bytes 1376264 | tf_op jit(solution)/shard_map/ppermute | solution.py:38
  32.2 22.0 %collective-permute-start.3 = (bf16[448,512]{1,0:T(8,128)(2,1)}, bf16[448,512]{1,0:T(8,128)(2,1)S(1)}, u32[]{:S(2)}, u32[]{:S(2)}) collective-permute-start(bf16[448,512]{1,0:T(8,128)(2,1)} %bitcast.17), channel_id=1, source_target_pairs={{0,1},{1,0},{2,3},{3,2},{4,5},{5,4},{6,7},{7,6},{8,9},{9,8},{10,11... | collective-permute-start | bytes 1376264 | tf_op jit(solution)/shard_map/ppermute | solution.py:38
  34.2 20.0 %collective-permute-start.1 = (bf16[448,512]{1,0:T(8,128)(2,1)}, bf16[448,512]{1,0:T(8,128)(2,1)S(1)}, u32[]{:S(2)}, u32[]{:S(2)}) collective-permute-start(bf16[448,512]{1,0:T(8,128)(2,1)} %bitcast.19), channel_id=1, source_target_pairs={{0,256},{256,0},{1,257},{257,1},{2,258},{258,2},{3,259},{259,3},{4... | collective-permute-start | bytes 1376264 | tf_op jit(solution)/shard_map/ppermute | solution.py:38
  36.6 17.6 %collective-permute-start.4 = (bf16[448,512]{1,0:T(8,128)(2,1)}, bf16[448,512]{1,0:T(8,128)(2,1)S(1)}, u32[]{:S(2)}, u32[]{:S(2)}) collective-permute-start(bf16[448,512]{1,0:T(8,128)(2,1)} %bitcast.20), channel_id=1, source_target_pairs={{0,1},{1,0},{2,3},{3,2},{4,5},{5,4},{6,7},{7,6},{8,9},{9,8},{10,11... | collective-permute-start | bytes 1376264 | tf_op jit(solution)/shard_map/ppermute | solution.py:38
  38.7 23.9 %collective-permute-start.2 = (bf16[448,512]{1,0:T(8,128)(2,1)}, bf16[448,512]{1,0:T(8,128)(2,1)}, u32[]{:S(2)}, u32[]{:S(2)}) collective-permute-start(bf16[448,512]{1,0:T(8,128)(2,1)} %refs_0_.1), channel_id=1, source_target_pairs={{0,256},{256,0},{1,257},{257,1},{2,258},{258,2},{3,259},{259,3},{4... | collective-permute-start | bytes 1376264 | tf_op jit(solution)/shard_map/ppermute | solution.py:38
  63.5 16.2 %copy-start = (bf16[512,448]{0,1:T(8,128)(2,1)S(1)}, bf16[512,448]{0,1:T(8,128)(2,1)}, u32[]{:S(2)}) copy-start(bf16[512,448]{0,1:T(8,128)(2,1)} %param.7) | copy-start | bytes 1376260
  63.5 16.2 %copy-start.1 = (bf16[512,448]{0,1:T(8,128)(2,1)S(1)}, bf16[512,448]{0,1:T(8,128)(2,1)}, u32[]{:S(2)}) copy-start(bf16[512,448]{0,1:T(8,128)(2,1)} %param.8) | copy-start | bytes 1376260
  63.5 16.2 %all-to-all-start.1 = ((bf16[8,64,512]{2,1,0:T(8,128)(2,1)}), bf16[8,64,512]{2,1,0:T(8,128)(2,1)S(1)}, u32[]{:S(2)}, u32[]{:S(2)}) async-start(bf16[8,64,512]{2,1,0:T(8,128)(2,1)} %bitcast.22), calls=%async_computation.1 | async-start | bytes 1048576 | tf_op jit(solution)/shard_map/all_to_all | solution.py:28
  68.8 5.4 %collective-permute-start.5 = (bf16[448,512]{1,0:T(8,128)(2,1)S(1)}, bf16[448,512]{1,0:T(8,128)(2,1)S(1)}, u32[]{:S(2)}, u32[]{:S(2)}) collective-permute-start(bf16[448,512]{1,0:T(8,128)(2,1)S(1)} %collective-permute-done.refs_2_), channel_id=1, source_target_pairs={{0,1},{1,0},{2,3},{3,2},{4,5},{5,4},{6,7},{7,6},{8,9},{9,8},{10,11... | collective-permute-start | bytes 1376264 | tf_op jit(solution)/shard_map/ppermute | solution.py:38
  72.2 3.7 %collective-permute-start.6 = (bf16[448,512]{1,0:T(8,128)(2,1)S(1)}, bf16[448,512]{1,0:T(8,128)(2,1)S(1)}, u32[]{:S(2)}, u32[]{:S(2)}) collective-permute-start(bf16[448,512]{1,0:T(8,128)(2,1)S(1)} %collective-permute-done.1.refs_3_), channel_id=1, source_target_pairs={{0,1},{1,0},{2,3},{3,2},{4,5},{5,4},{6,7},{7,6},{8,9},{9,8},{10,11... | collective-permute-start | bytes 1376264 | tf_op jit(solution)/shard_map/ppermute | solution.py:38
  74.2 0.8 copy-start.2
  76.0 0.8 copy-start.4
  79.7 1.0 copy-start.3
  80.8 1.0 copy-start.5
  84.0 8.7 %copy-start.6 = (bf16[448,512]{1,0:T(8,128)(2,1)S(1)}, bf16[448,512]{1,0:T(8,128)(2,1)}, u32[]{:S(2)}) copy-start(bf16[448,512]{1,0:T(8,128)(2,1)} %refs_0_.1) | copy-start | bytes 1376260
  84.0 20.0 %all-to-all-start.2 = ((bf16[8,32,1792]{2,1,0:T(8,128)(2,1)}), bf16[8,32,1792]{2,1,0:T(8,128)(2,1)S(1)}, u32[]{:S(2)}, u32[]{:S(2)}) async-start(bf16[8,32,1792]{2,1,0:T(8,128)(2,1)} %bitcast.7), calls=%async_computation.2 | async-start | bytes 1835008 | tf_op jit(solution)/shard_map/all_to_all | solution.py:24
  90.8 17.8 %collective-permute-start.8 = (bf16[448,512]{1,0:T(8,128)(2,1)}, bf16[448,512]{1,0:T(8,128)(2,1)S(1)}, u32[]{:S(2)}, u32[]{:S(2)}) collective-permute-start(bf16[448,512]{1,0:T(8,128)(2,1)} %collective-permute-done.2.refs_1_), channel_id=1, source_target_pairs={{0,1},{1,0},{2,3},{3,2},{4,5},{5,4},{6,7},{7,6},{8,9},{9,8},{10,11... | collective-permute-start | bytes 1376264 | tf_op jit(solution)/shard_map/ppermute | solution.py:38
  92.7 15.9 %collective-permute-start.7 = (bf16[448,512]{1,0:T(8,128)(2,1)S(1)}, bf16[448,512]{1,0:T(8,128)(2,1)S(1)}, u32[]{:S(2)}, u32[]{:S(2)}) collective-permute-start(bf16[448,512]{1,0:T(8,128)(2,1)S(1)} %copy-done.6), channel_id=1, source_target_pairs={{0,1},{1,0},{2,3},{3,2},{4,5},{5,4},{6,7},{7,6},{8,9},{9,8},{10,11... | collective-permute-start | bytes 1376264 | tf_op jit(solution)/shard_map/ppermute | solution.py:38
  105.0 14.4 %all-to-all-start.3 = ((bf16[8,2,32,448]{3,2,1,0:T(8,128)(2,1)}), bf16[8,2,32,448]{3,2,1,0:T(8,128)(2,1)S(1)}, u32[]{:S(2)}, u32[]{:S(2)}) async-start(bf16[8,2,32,448]{3,2,1,0:T(8,128)(2,1)} %shard_map.56), calls=%async_computation.3 | async-start | bytes 1048576 | tf_op jit(solution)/shard_map/all_to_all | solution.py:24
  139.2 47.2 %all-to-all-start.5 = ((bf16[8,16,512]{2,1,0:T(8,128)(2,1)}), bf16[8,16,512]{2,1,0:T(8,128)(2,1)S(1)}, u32[]{:S(2)}, u32[]{:S(2)}) async-start(bf16[8,16,512]{2,1,0:T(8,128)(2,1)} %shard_map.58), calls=%async_computation.5 | async-start | bytes 262144 | tf_op jit(solution)/shard_map/all_to_all | solution.py:24
  157.6 0.7 copy-start.7

commit v7 on v5

--- a/solution.py
+++ b/solution.py
@@ -112,6 +112,40 @@
     )(hidden, downs)
 
 
+def near_sum_kernel(parts_ref, out_ref):
+    feats = parts_ref.shape[2]
+    sums = []
+    for xl in range(XL):
+        total = jnp.sum(parts_ref[xl * ZL : (xl + 1) * ZL].astype(F32), axis=0)
+        sums.append(total.reshape(ZH, -1, feats))
+    out_ref[...] = jnp.concatenate(sums, axis=1).astype(BF16)
+
+
+def near_sum(parts):
+    return pl.pallas_call(
+        near_sum_kernel,
+        out_shape=jax.ShapeDtypeStruct((ZH, XL * parts.shape[1] // ZH, parts.shape[2]), BF16),
+        in_specs=[VMEM],
+        out_specs=VMEM,
+        compiler_params=PARAMS,
+    )(parts)
+
+
+def far_sum_kernel(parts_ref, mask_ref, out_ref):
+    total = jnp.sum(parts_ref[...].astype(F32), axis=0)
+    out_ref[...] = (total * mask_ref[...].astype(F32)).astype(BF16)
+
+
+def far_sum(parts, mask):
+    return pl.pallas_call(
+        far_sum_kernel,
+        out_shape=jax.ShapeDtypeStruct(parts.shape[1:], BF16),
+        in_specs=[VMEM, VMEM],
+        out_specs=VMEM,
+        compiler_params=PARAMS,
+    )(parts, mask)
+
+
 def on_device(tokens, pad_mask, gate_weight, up_weight, down_weight):
     rows, feats = tokens.shape
     width = gate_weight.shape[1]
@@ -127,6 +161,7 @@
     far = far.reshape(ZH, XL, sub, feats).transpose(1, 0, 2, 3).reshape(XL, 1, some, feats)
     far = jnp.broadcast_to(far, (XL, ZL, some, feats)).reshape(XL * ZL, some, feats)
     own = near_exchange(far).reshape(XL, ZL, some, feats)
+    own, mask = lax.optimization_barrier((own, pad_mask[:, None]))
     weights = (mine, beside, mine_other, beside_other)
 
     groups = XP * Y
@@ -135,12 +170,9 @@
     sums = exchange(sums.reshape(groups, few, C * 2 * width), ("xp", "y"))
     hidden = exchange(activate(sums, groups), ("xp", "y"))
 
-    part = second(hidden, downs).reshape(XL * ZL, some, feats)
-    part = near_exchange(part).reshape(XL, ZL, some, feats)
-    part = jnp.sum(part.astype(F32), axis=1).astype(BF16)
-    part = part.reshape(XL, ZH, sub, feats).transpose(1, 0, 2, 3).reshape(ZH, rows, feats)
-    result = jnp.sum(exchange(part, "zh").astype(F32), axis=0)
-    return (result * pad_mask[:, None].astype(F32)).astype(BF16)
+    part = near_exchange(second(hidden, downs).reshape(XL * ZL, some, feats))
+    part = exchange(near_sum(part), "zh")
+    return far_sum(part, mask)
 
 
 def solution(mesh):

time: 169 us -> 168 us (level)
  local copies, waits for them, and re-layouts: 6.43 us -> 0.96 us
  Pallas kernels: 2.15 us -> 5.39 us
  waiting for transfers between devices: 32.1 us -> 34.3 us
    unnamed x12 -> x4, local copies, waits for them, and re-layouts: 4.89 us -> 0.01 us
    all_to_all x1, waiting for transfers between devices: 1.98 us -> 6.17 us  [near_exchange(): lax.all_to_all(pieces, ('xl',) + DP, split_axis=0, concat_axis=0, tiled=T...]
    ppermute x3, waiting for transfers between devices: 1.99 us -> 0.01 us  [swap(): return lax.ppermute(block, axis, [(0, 1), (1, 0)])]
    pallas_call x1, Pallas kernels: 1.3 us -> 3.15 us  [first(): pl.pallas_call(first_kernel, out_shape=(jax.ShapeDtypeStruct((rows, C * 2...]
  transfers between devices with their start and end apart: 5 -> 5, of which waited for: 4 -> 2; matrix products, arithmetic and copies ran while one was open for 0% -> 0% of each run, Pallas kernels for 0% -> 0%
where the time goes in v7:
time: 168 us; the launch traced here: 167 us
  blocking collectives  95.5 us (57%)
  waiting for transfers between devices  34.3 us (20%)
  starting transfers between devices  29.6 us (18%)
  Pallas kernels  5.39 us (3%)
    all_to_all x3, blocking collectives, exchange(): return lax.all_to_all(pieces, axes, split_axis=0, concat_axis=0, tiled=True)  76.4 us
    all_to_all x1, waiting for transfers between devices, exchange(): return lax.all_to_all(pieces, axes, split_axis=0, concat_axis=0, tiled=True)  28.1 us
    ppermute x3, starting transfers between devices, swap(): return lax.ppermute(block, axis, [(0, 1), (1, 0)])  19.6 us
    all_to_all x1, blocking collectives, near_exchange(): lax.all_to_all(pieces, ('xl',) + DP, split_axis=0, concat_axis=0, tiled=T...  19 us
    all_to_all x1, starting transfers between devices, near_exchange(): lax.all_to_all(pieces, ('xl',) + DP, split_axis=0, concat_axis=0, tiled=T...  6.27 us
    all_to_all x1, waiting for transfers between devices, near_exchange(): lax.all_to_all(pieces, ('xl',) + DP, split_axis=0, concat_axis=0, tiled=T...  6.17 us
    all_to_all x1, starting transfers between devices, exchange(): return lax.all_to_all(pieces, axes, split_axis=0, concat_axis=0, tiled=True)  3.67 us
  transfers between devices with their start and end apart: 5, of which 2 were waited for; matrix products, arithmetic and copies ran while one was open for 0% of the time, Pallas kernels for 0%

profile of v7, /device:TPU:2, one launch (start us, length us, event | category | flops | bytes accessed | tf_op | source)
XLA Modules:
  0.0 167.2 jit_solution(16115544093227081594)
XLA Ops:
  0.0 0.0 copy-start
  0.0 1.5 pad_maximum_fusion.mine
  1.5 15.1 %collective-permute-start = (bf16[3,448,512]{2,1,0:T(8,128)(2,1)S(1)}, bf16[3,448,512]{2,1,0:T(8,128)(2,1)S(1)}, u32[]{:S(2)}, u32[]{:S(2)}) collective-permute-start(bf16[3,448,512]{2,1,0:T(8,128)(2,1)S(1)} %pad_maximum_fusion.mine), channel_id=1, source_target_pairs={{0,256},{256,0},{1,257},{257,1},{2,258},{258,2},{3,259},{259,3},{4... | collective-permute-start | bytes 4128776 | tf_op jit(solution)/shard_map/ppermute | solution.py:38
  16.6 0.0 copy-done
  16.6 43.3 %all_to_all.30 = bf16[8,16,512]{2,1,0:T(8,128)(2,1)S(1)} all-to-all(bf16[8,16,512]{2,1,0:T(8,128)(2,1)S(1)} %broadcast_in_dim.16), channel_id=1, replica_groups=mesh['xp'=2,'xl'=2,'y'=4,'zh'=8,'zl'=4,'c'=2] {'zh'}, dimensions={0} | all-to-all | bytes 262144 | tf_op jit(solution)/shard_map/all_to_all | solution.py:24
  59.9 0.0 collective-permute-done.beside
  59.9 0.8 broadcast_in_dim.18
  60.7 6.3 %all-to-all-start.1 = ((bf16[8,64,512]{2,1,0:T(8,128)(2,1)}), bf16[8,64,512]{2,1,0:T(8,128)(2,1)S(1)}, u32[]{:S(2)}, u32[]{:S(2)}) async-start(bf16[8,64,512]{2,1,0:T(8,128)(2,1)} %bitcast.22), calls=%async_computation.1 | async-start | bytes 1048576 | tf_op jit(solution)/shard_map/all_to_all | solution.py:28
  67.0 2.6 %collective-permute-start.1 = (bf16[3,448,512]{2,1,0:T(8,128)(2,1)S(1)}, bf16[3,448,512]{2,1,0:T(8,128)(2,1)}, u32[]{:S(2)}, u32[]{:S(2)}) collective-permute-start(bf16[3,448,512]{2,1,0:T(8,128)(2,1)S(1)} %pad_maximum_fusion.mine), channel_id=1, source_target_pairs={{0,1},{1,0},{2,3},{3,2},{4,5},{5,4},{6,7},{7,6},{8,9},{9,8},{10,11... | collective-permute-start | bytes 4128776 | tf_op jit(solution)/shard_map/ppermute | solution.py:38
  69.6 1.9 %collective-permute-start.2 = (bf16[3,448,512]{2,1,0:T(8,128)(2,1)S(1)}, bf16[3,448,512]{2,1,0:T(8,128)(2,1)}, u32[]{:S(2)}, u32[]{:S(2)}) collective-permute-start(bf16[3,448,512]{2,1,0:T(8,128)(2,1)S(1)} %collective-permute-done.beside), channel_id=1, source_target_pairs={{0,1},{1,0},{2,3},{3,2},{4,5},{5,4},{6,7},{7,6},{8,9},{9,8},{10,11... | collective-permute-start | bytes 4128776 | tf_op jit(solution)/shard_map/ppermute | solution.py:38
  71.6 6.2 %all-to-all-done.1 = bf16[8,64,512]{2,1,0:T(8,128)(2,1)S(1)} async-done(((bf16[8,64,512]{2,1,0:T(8,128)(2,1)}), bf16[8,64,512]{2,1,0:T(8,128)(2,1)S(1)}, u32[]{:S(2)}, u32[]{:S(2)}) %all-to-all-start.1) | async-done | bytes 524320 | tf_op jit(solution)/shard_map/all_to_all | solution.py:28
  77.7 0.0 collective-permute-done.1.mine_other
  77.7 0.0 collective-permute-done.2.beside_other
  77.7 3.1 %shard_map.55 = (bf16[256,1792]{1,0:T(8,128)(2,1)S(1)}, bf16[4,448,512]{2,1,0:T(8,128)(2,1)S(1)}) custom-call(bf16[2,4,64,512]{3,2,1,0:T(8,128)(2,1)S(1)} %bitcast.19, bf16[3,448,512]{2,1,0:T(8,128)(2,1)S(1)} %pad_maximum_fusion.mine, bf16[3,448,512]{2,1,0:T(8,128)(2,1)S(1)} %collective-permute-done.beside, ...), custom_call_target="tpu_custom_call" | custom-call | tf_op jit(solution)/shard_map/pallas_call | solution.py:60
  80.9 20.6 %all_to_all.31.sums_ref = bf16[8,32,1792]{2,1,0:T(8,128)(2,1)S(1)} all-to-all(bf16[8,32,1792]{2,1,0:T(8,128)(2,1)S(1)} %bitcast.21), channel_id=1, replica_groups=mesh['xp'=2,'xl'=2,'y'=4,'zh'=8,'zl'=4,'c'=2] {'xp','y'}, dimensions={0} | all-to-all | bytes 1835008 | tf_op jit(solution)/shard_map/all_to_all | solution.py:24
  101.4 0.1 shard_map.56
  101.6 12.6 %all_to_all.32.hidden_ref = bf16[8,2,32,448]{3,2,1,0:T(8,128)(2,1)S(1)} all-to-all(bf16[8,2,32,448]{3,2,1,0:T(8,128)(2,1)S(1)} %shard_map.56), channel_id=1, replica_groups=mesh['xp'=2,'xl'=2,'y'=4,'zh'=8,'zl'=4,'c'=2] {'xp','y'}, dimensions={0} | all-to-all | bytes 917504 | tf_op jit(solution)/shard_map/all_to_all | solution.py:24
  114.2 0.7 shard_map.57
  114.9 0.0 copy-start.1
  114.9 19.0 %all_to_all.33.parts_ref = bf16[8,64,512]{2,1,0:T(8,128)(2,1)S(1)} all-to-all(bf16[8,64,512]{2,1,0:T(8,128)(2,1)S(1)} %bitcast.20), channel_id=1, replica_groups={{0,2,4,6,256,258,260,262},{8,10,12,14,264,266,268,270},{16,18,20,22,272..., dimensions={0} | all-to-all | bytes 1048576 | tf_op jit(solution)/shard_map/all_to_all | solution.py:28
  134.0 0.7 shard_map.58
  134.7 3.7 %all-to-all-start.5 = ((bf16[8,16,512]{2,1,0:T(8,128)(2,1)}), bf16[8,16,512]{2,1,0:T(8,128)(2,1)S(1)}, u32[]{:S(2)}, u32[]{:S(2)}) async-start(bf16[8,16,512]{2,1,0:T(8,128)(2,1)} %shard_map.58), calls=%async_computation.5 | async-start | bytes 262144 | tf_op jit(solution)/shard_map/all_to_all | solution.py:24
  138.4 0.0 copy-done.1
  138.4 0.1 copy.9.mask_ref
  138.4 28.1 %all-to-all-done.5.parts_ref = bf16[8,16,512]{2,1,0:T(8,128)(2,1)S(1)} async-done(((bf16[8,16,512]{2,1,0:T(8,128)(2,1)}), bf16[8,16,512]{2,1,0:T(8,128)(2,1)S(1)}, u32[]{:S(2)}, u32[]{:S(2)}) %all-to-all-start.5) | async-done | bytes 131104 | tf_op jit(solution)/shard_map/all_to_all | solution.py:24
  166.5 0.7 shard_map.59
  (2 shorter events, 0.0 us)
Async XLA Ops:
  0.0 16.6 %copy-start = (bf16[16,512]{1,0:T(8,128)(2,1)S(1)}, bf16[16,512]{1,0:T(8,128)(2,1)}, u32[]{:S(2)}) copy-start(bf16[16,512]{1,0:T(8,128)(2,1)} %param.5) | copy-start | bytes 49156
  1.5 58.4 %collective-permute-start = (bf16[3,448,512]{2,1,0:T(8,128)(2,1)S(1)}, bf16[3,448,512]{2,1,0:T(8,128)(2,1)S(1)}, u32[]{:S(2)}, u32[]{:S(2)}) collective-permute-start(bf16[3,448,512]{2,1,0:T(8,128)(2,1)S(1)} %pad_maximum_fusion.mine), channel_id=1, source_target_pairs={{0,256},{256,0},{1,257},{257,1},{2,258},{258,2},{3,259},{259,3},{4... | collective-permute-start | bytes 4128776 | tf_op jit(solution)/shard_map/ppermute | solution.py:38
  60.7 17.0 %all-to-all-start.1 = ((bf16[8,64,512]{2,1,0:T(8,128)(2,1)}), bf16[8,64,512]{2,1,0:T(8,128)(2,1)S(1)}, u32[]{:S(2)}, u32[]{:S(2)}) async-start(bf16[8,64,512]{2,1,0:T(8,128)(2,1)} %bitcast.22), calls=%async_computation.1 | async-start | bytes 1048576 | tf_op jit(solution)/shard_map/all_to_all | solution.py:28
  67.0 10.7 %collective-permute-start.1 = (bf16[3,448,512]{2,1,0:T(8,128)(2,1)S(1)}, bf16[3,448,512]{2,1,0:T(8,128)(2,1)}, u32[]{:S(2)}, u32[]{:S(2)}) collective-permute-start(bf16[3,448,512]{2,1,0:T(8,128)(2,1)S(1)} %pad_maximum_fusion.mine), channel_id=1, source_target_pairs={{0,1},{1,0},{2,3},{3,2},{4,5},{5,4},{6,7},{7,6},{8,9},{9,8},{10,11... | collective-permute-start | bytes 4128776 | tf_op jit(solution)/shard_map/ppermute | solution.py:38
  69.6 8.1 %collective-permute-start.2 = (bf16[3,448,512]{2,1,0:T(8,128)(2,1)S(1)}, bf16[3,448,512]{2,1,0:T(8,128)(2,1)}, u32[]{:S(2)}, u32[]{:S(2)}) collective-permute-start(bf16[3,448,512]{2,1,0:T(8,128)(2,1)S(1)} %collective-permute-done.beside), channel_id=1, source_target_pairs={{0,1},{1,0},{2,3},{3,2},{4,5},{5,4},{6,7},{7,6},{8,9},{9,8},{10,11... | collective-permute-start | bytes 4128776 | tf_op jit(solution)/shard_map/ppermute | solution.py:38
  114.9 23.4 %copy-start.1 = (s32[16]{0:T(128)S(1)}, s32[16]{0:T(128)}, u32[]{:S(2)}) copy-start(s32[16]{0:T(128)} %param.6) | copy-start | bytes 196
  134.7 31.8 %all-to-all-start.5 = ((bf16[8,16,512]{2,1,0:T(8,128)(2,1)}), bf16[8,16,512]{2,1,0:T(8,128)(2,1)S(1)}, u32[]{:S(2)}, u32[]{:S(2)}) async-start(bf16[8,16,512]{2,1,0:T(8,128)(2,1)} %shard_map.58), calls=%async_computation.5 | async-start | bytes 262144 | tf_op jit(solution)/shard_map/all_to_all | solution.py:24

commit v8 on v7

--- a/solution.py
+++ b/solution.py
@@ -133,14 +133,18 @@
 
 def far_sum_kernel(parts_ref, mask_ref, out_ref):
     total = jnp.sum(parts_ref[...].astype(F32), axis=0)
-    out_ref[...] = (total * mask_ref[...].astype(F32)).astype(BF16)
+    row = lax.broadcasted_iota(jnp.int32, (total.shape[0], 1), 0)
+    mask = jnp.zeros_like(row)
+    for i in range(total.shape[0]):
+        mask = jnp.where(row == i, mask_ref[i], mask)
+    out_ref[...] = (total * mask.astype(F32)).astype(BF16)
 
 
 def far_sum(parts, mask):
     return pl.pallas_call(
         far_sum_kernel,
         out_shape=jax.ShapeDtypeStruct(parts.shape[1:], BF16),
-        in_specs=[VMEM, VMEM],
+        in_specs=[VMEM, pl.BlockSpec(memory_space=pltpu.SMEM)],
         out_specs=VMEM,
         compiler_params=PARAMS,
     )(parts, mask)
@@ -161,7 +165,7 @@
     far = far.reshape(ZH, XL, sub, feats).transpose(1, 0, 2, 3).reshape(XL, 1, some, feats)
     far = jnp.broadcast_to(far, (XL, ZL, some, feats)).reshape(XL * ZL, some, feats)
     own = near_exchange(far).reshape(XL, ZL, some, feats)
-    own, mask = lax.optimization_barrier((own, pad_mask[:, None]))
+    own, mask = lax.optimization_barrier((own, pad_mask))
     weights = (mine, beside, mine_other, beside_other)
 
     groups = XP * Y

time: 168 us -> 167 us (level)
  the two profiles are of different devices: /device:TPU:2 before, /device:TPU:8 now
where the time goes in v8:
time: 167 us
  blocking collectives  139 us (83%)
  starting transfers between devices  13.3 us (8%)
  waiting for transfers between devices  7.08 us (4%)
  Pallas kernels  5.24 us (3%)
    all_to_all x4, blocking collectives, exchange(): return lax.all_to_all(pieces, axes, split_axis=0, concat_axis=0, tiled=True)  119 us
    all_to_all x1, blocking collectives, near_exchange(): lax.all_to_all(pieces, ('xl',) + DP, split_axis=0, concat_axis=0, tiled=T...  19.6 us
    ppermute x3, starting transfers between devices, swap(): return lax.ppermute(block, axis, [(0, 1), (1, 0)])  8.5 us
    all_to_all x1, waiting for transfers between devices, near_exchange(): lax.all_to_all(pieces, ('xl',) + DP, split_axis=0, concat_axis=0, tiled=T...  7.08 us
    all_to_all x1, starting transfers between devices, near_exchange(): lax.all_to_all(pieces, ('xl',) + DP, split_axis=0, concat_axis=0, tiled=T...  4.78 us
  transfers between devices with their start and end apart: 4, of which 1 were waited for; matrix products, arithmetic and copies ran while one was open for 0% of the time, Pallas kernels for 0%

profile of v8, /device:TPU:8, one launch (start us, length us, event | category | flops | bytes accessed | tf_op | source)
XLA Modules:
  0.0 166.9 jit_solution(6316622727503731532)
XLA Ops:
  0.0 0.0 copy-start.1
  0.0 1.5 pad_maximum_fusion.mine
  1.5 3.4 %collective-permute-start = (bf16[3,448,512]{2,1,0:T(8,128)(2,1)S(1)}, bf16[3,448,512]{2,1,0:T(8,128)(2,1)S(1)}, u32[]{:S(2)}, u32[]{:S(2)}) collective-permute-start(bf16[3,448,512]{2,1,0:T(8,128)(2,1)S(1)} %pad_maximum_fusion.mine), channel_id=1, source_target_pairs={{0,256},{256,0},{1,257},{257,1},{2,258},{258,2},{3,259},{259,3},{4... | collective-permute-start | bytes 4128776 | tf_op jit(solution)/shard_map/ppermute | solution.py:38
  4.9 0.0 copy-done.1
  4.9 55.9 %all_to_all.30 = bf16[8,16,512]{2,1,0:T(8,128)(2,1)S(1)} all-to-all(bf16[8,16,512]{2,1,0:T(8,128)(2,1)S(1)} %broadcast_in_dim.6), channel_id=1, replica_groups=mesh['xp'=2,'xl'=2,'y'=4,'zh'=8,'zl'=4,'c'=2] {'zh'}, dimensions={0} | all-to-all | bytes 262144 | tf_op jit(solution)/shard_map/all_to_all | solution.py:24
  60.8 0.0 collective-permute-done.beside
  60.8 0.9 broadcast_in_dim.15
  61.7 4.8 %all-to-all-start.1 = ((bf16[8,64,512]{2,1,0:T(8,128)(2,1)}), bf16[8,64,512]{2,1,0:T(8,128)(2,1)S(1)}, u32[]{:S(2)}, u32[]{:S(2)}) async-start(bf16[8,64,512]{2,1,0:T(8,128)(2,1)} %bitcast.21), calls=%async_computation.1 | async-start | bytes 1048576 | tf_op jit(solution)/shard_map/all_to_all | solution.py:28
  66.5 3.2 %collective-permute-start.1 = (bf16[3,448,512]{2,1,0:T(8,128)(2,1)S(1)}, bf16[3,448,512]{2,1,0:T(8,128)(2,1)}, u32[]{:S(2)}, u32[]{:S(2)}) collective-permute-start(bf16[3,448,512]{2,1,0:T(8,128)(2,1)S(1)} %pad_maximum_fusion.mine), channel_id=1, source_target_pairs={{0,1},{1,0},{2,3},{3,2},{4,5},{5,4},{6,7},{7,6},{8,9},{9,8},{10,11... | collective-permute-start | bytes 4128776 | tf_op jit(solution)/shard_map/ppermute | solution.py:38
  69.7 1.9 %collective-permute-start.2 = (bf16[3,448,512]{2,1,0:T(8,128)(2,1)S(1)}, bf16[3,448,512]{2,1,0:T(8,128)(2,1)}, u32[]{:S(2)}, u32[]{:S(2)}) collective-permute-start(bf16[3,448,512]{2,1,0:T(8,128)(2,1)S(1)} %collective-permute-done.beside), channel_id=1, source_target_pairs={{0,1},{1,0},{2,3},{3,2},{4,5},{5,4},{6,7},{7,6},{8,9},{9,8},{10,11... | collective-permute-start | bytes 4128776 | tf_op jit(solution)/shard_map/ppermute | solution.py:38
  71.6 7.1 %all-to-all-done.1 = bf16[8,64,512]{2,1,0:T(8,128)(2,1)S(1)} async-done(((bf16[8,64,512]{2,1,0:T(8,128)(2,1)}), bf16[8,64,512]{2,1,0:T(8,128)(2,1)S(1)}, u32[]{:S(2)}, u32[]{:S(2)}) %all-to-all-start.1) | async-done | bytes 524320 | tf_op jit(solution)/shard_map/all_to_all | solution.py:28
  78.7 0.0 collective-permute-done.1.mine_other
  78.7 0.0 collective-permute-done.2.beside_other
  78.7 3.1 %shard_map.55 = (bf16[256,1792]{1,0:T(8,128)(2,1)S(1)}, bf16[4,448,512]{2,1,0:T(8,128)(2,1)S(1)}) custom-call(bf16[2,4,64,512]{3,2,1,0:T(8,128)(2,1)S(1)} %bitcast.18, bf16[3,448,512]{2,1,0:T(8,128)(2,1)S(1)} %pad_maximum_fusion.mine, bf16[3,448,512]{2,1,0:T(8,128)(2,1)S(1)} %collective-permute-done.beside, ...), custom_call_target="tpu_custom_call" | custom-call | tf_op jit(solution)/shard_map/pallas_call | solution.py:60
  81.8 18.9 %all_to_all.31.sums_ref = bf16[8,32,1792]{2,1,0:T(8,128)(2,1)S(1)} all-to-all(bf16[8,32,1792]{2,1,0:T(8,128)(2,1)S(1)} %bitcast.20), channel_id=1, replica_groups=mesh['xp'=2,'xl'=2,'y'=4,'zh'=8,'zl'=4,'c'=2] {'xp','y'}, dimensions={0} | all-to-all | bytes 1835008 | tf_op jit(solution)/shard_map/all_to_all | solution.py:24
  100.7 0.1 shard_map.56
  100.8 12.4 %all_to_all.32.hidden_ref = bf16[8,2,32,448]{3,2,1,0:T(8,128)(2,1)S(1)} all-to-all(bf16[8,2,32,448]{3,2,1,0:T(8,128)(2,1)S(1)} %shard_map.56), channel_id=1, replica_groups=mesh['xp'=2,'xl'=2,'y'=4,'zh'=8,'zl'=4,'c'=2] {'xp','y'}, dimensions={0} | all-to-all | bytes 917504 | tf_op jit(solution)/shard_map/all_to_all | solution.py:24
  113.2 0.7 shard_map.57
  113.9 0.0 copy-start
  113.9 19.6 %all_to_all.33.parts_ref = bf16[8,64,512]{2,1,0:T(8,128)(2,1)S(1)} all-to-all(bf16[8,64,512]{2,1,0:T(8,128)(2,1)S(1)} %bitcast.19), channel_id=1, replica_groups={{0,2,4,6,256,258,260,262},{8,10,12,14,264,266,268,270},{16,18,20,22,272..., dimensions={0} | all-to-all | bytes 1048576 | tf_op jit(solution)/shard_map/all_to_all | solution.py:28
  133.5 0.1 shard_map.58
  133.6 32.1 %all_to_all.34.parts_ref = bf16[8,16,512]{2,1,0:T(8,128)(2,1)S(1)} all-to-all(bf16[8,16,512]{2,1,0:T(8,128)(2,1)S(1)} %shard_map.58), channel_id=1, replica_groups=mesh['xp'=2,'xl'=2,'y'=4,'zh'=8,'zl'=4,'c'=2] {'zh'}, dimensions={0} | all-to-all | bytes 262144 | tf_op jit(solution)/shard_map/all_to_all | solution.py:24
  165.7 0.0 copy-done
  165.7 1.2 shard_map.59
  (2 shorter events, 0.0 us)
Async XLA Ops:
  0.0 4.9 %copy-start.1 = (bf16[16,512]{1,0:T(8,128)(2,1)S(1)}, bf16[16,512]{1,0:T(8,128)(2,1)}, u32[]{:S(2)}) copy-start(bf16[16,512]{1,0:T(8,128)(2,1)} %param.5) | copy-start | bytes 49156
  1.5 59.4 %collective-permute-start = (bf16[3,448,512]{2,1,0:T(8,128)(2,1)S(1)}, bf16[3,448,512]{2,1,0:T(8,128)(2,1)S(1)}, u32[]{:S(2)}, u32[]{:S(2)}) collective-permute-start(bf16[3,448,512]{2,1,0:T(8,128)(2,1)S(1)} %pad_maximum_fusion.mine), channel_id=1, source_target_pairs={{0,256},{256,0},{1,257},{257,1},{2,258},{258,2},{3,259},{259,3},{4... | collective-permute-start | bytes 4128776 | tf_op jit(solution)/shard_map/ppermute | solution.py:38
  61.7 17.0 %all-to-all-start.1 = ((bf16[8,64,512]{2,1,0:T(8,128)(2,1)}), bf16[8,64,512]{2,1,0:T(8,128)(2,1)S(1)}, u32[]{:S(2)}, u32[]{:S(2)}) async-start(bf16[8,64,512]{2,1,0:T(8,128)(2,1)} %bitcast.21), calls=%async_computation.1 | async-start | bytes 1048576 | tf_op jit(solution)/shard_map/all_to_all | solution.py:28
  66.5 12.2 %collective-permute-start.1 = (bf16[3,448,512]{2,1,0:T(8,128)(2,1)S(1)}, bf16[3,448,512]{2,1,0:T(8,128)(2,1)}, u32[]{:S(2)}, u32[]{:S(2)}) collective-permute-start(bf16[3,448,512]{2,1,0:T(8,128)(2,1)S(1)} %pad_maximum_fusion.mine), channel_id=1, source_target_pairs={{0,1},{1,0},{2,3},{3,2},{4,5},{5,4},{6,7},{7,6},{8,9},{9,8},{10,11... | collective-permute-start | bytes 4128776 | tf_op jit(solution)/shard_map/ppermute | solution.py:38
  69.7 9.0 %collective-permute-start.2 = (bf16[3,448,512]{2,1,0:T(8,128)(2,1)S(1)}, bf16[3,448,512]{2,1,0:T(8,128)(2,1)}, u32[]{:S(2)}, u32[]{:S(2)}) collective-permute-start(bf16[3,448,512]{2,1,0:T(8,128)(2,1)S(1)} %collective-permute-done.beside), channel_id=1, source_target_pairs={{0,1},{1,0},{2,3},{3,2},{4,5},{5,4},{6,7},{7,6},{8,9},{9,8},{10,11... | collective-permute-start | bytes 4128776 | tf_op jit(solution)/shard_map/ppermute | solution.py:38
  113.9 51.8 %copy-start = (s32[16]{0:T(128)S(1)}, s32[16]{0:T(128)}, u32[]{:S(2)}) copy-start(s32[16]{0:T(128)} %mask_ref) | copy-start | bytes 196

commit v9 on v8

--- a/solution.py
+++ b/solution.py
@@ -8,7 +8,7 @@
 XP, XL, Y, ZH, ZL, C = 2, 2, 4, 8, 4, 2
 Z = ZH * ZL
 DP = ("zh", "zl", "c")
-TENSOR = ("xp", "xl", "y")
+TENSOR = ("xl", "xp", "y")
 NEAR = [
     [(xl * Z + (first * ZL + core * ZL // 2 + step) % Z) * C + core for xl in range(XL) for step in range(ZL)]
     for core in range(C)
@@ -180,7 +180,7 @@
 
 
 def solution(mesh):
-    fine = Mesh(mesh.devices.reshape(XP, XL, Y, ZH, ZL, C), TENSOR + DP)
+    fine = Mesh(mesh.devices.reshape(XL, XP, Y, ZH, ZL, C), TENSOR + DP)
     placed = (P(DP, TENSOR), P(DP), P(TENSOR, DP), P(TENSOR, DP), P(DP, TENSOR))
     return jax.shard_map(
         on_device, mesh=fine, in_specs=placed, out_specs=P(DP, TENSOR), check_vma=False

time: 167 us -> 167 us (level)
  the two profiles are of different devices: /device:TPU:8 before, /device:TPU:2 now
where the time goes in v9:
time: 167 us
  blocking collectives  135 us (81%)
  starting transfers between devices  14.8 us (9%)
  waiting for transfers between devices  8.8 us (5%)
  Pallas kernels  5.24 us (3%)
    all_to_all x4, blocking collectives, exchange(): return lax.all_to_all(pieces, axes, split_axis=0, concat_axis=0, tiled=True)  114 us
    all_to_all x1, blocking collectives, near_exchange(): lax.all_to_all(pieces, ('xl',) + DP, split_axis=0, concat_axis=0, tiled=T...  21.1 us
    ppermute x3, starting transfers between devices, swap(): return lax.ppermute(block, axis, [(0, 1), (1, 0)])  9.13 us
    all_to_all x1, waiting for transfers between devices, near_exchange(): lax.all_to_all(pieces, ('xl',) + DP, split_axis=0, concat_axis=0, tiled=T...  8.79 us
    all_to_all x1, starting transfers between devices, near_exchange(): lax.all_to_all(pieces, ('xl',) + DP, split_axis=0, concat_axis=0, tiled=T...  5.62 us
  transfers between devices with their start and end apart: 4, of which 1 were waited for; matrix products, arithmetic and copies ran while one was open for 0% of the time, Pallas kernels for 0%

profile of v9, /device:TPU:2, one launch (start us, length us, event | category | flops | bytes accessed | tf_op | source)
XLA Modules:
  0.0 166.7 jit_solution(2527318583425060600)
XLA Ops:
  0.0 0.0 copy-start.1
  0.0 1.5 pad_maximum_fusion.mine
  1.5 4.0 %collective-permute-start = (bf16[3,448,512]{2,1,0:T(8,128)(2,1)S(1)}, bf16[3,448,512]{2,1,0:T(8,128)(2,1)S(1)}, u32[]{:S(2)}, u32[]{:S(2)}) collective-permute-start(bf16[3,448,512]{2,1,0:T(8,128)(2,1)S(1)} %pad_maximum_fusion.mine), channel_id=1, source_target_pairs={{0,512},{512,0},{1,513},{513,1},{2,514},{514,2},{3,515},{515,3},{4... | collective-permute-start | bytes 4128776 | tf_op jit(solution)/shard_map/ppermute | solution.py:38
  5.5 0.0 copy-done.1
  5.5 55.9 %all_to_all.30 = bf16[8,16,512]{2,1,0:T(8,128)(2,1)S(1)} all-to-all(bf16[8,16,512]{2,1,0:T(8,128)(2,1)S(1)} %broadcast_in_dim.6), channel_id=1, replica_groups=mesh['xl'=2,'xp'=2,'y'=4,'zh'=8,'zl'=4,'c'=2] {'zh'}, dimensions={0} | all-to-all | bytes 262144 | tf_op jit(solution)/shard_map/all_to_all | solution.py:24
  61.5 0.0 collective-permute-done.beside
  61.5 0.9 broadcast_in_dim.15
  62.3 5.6 %all-to-all-start.1 = ((bf16[8,64,512]{2,1,0:T(8,128)(2,1)}), bf16[8,64,512]{2,1,0:T(8,128)(2,1)S(1)}, u32[]{:S(2)}, u32[]{:S(2)}) async-start(bf16[8,64,512]{2,1,0:T(8,128)(2,1)} %bitcast.21), calls=%async_computation.1 | async-start | bytes 1048576 | tf_op jit(solution)/shard_map/all_to_all | solution.py:28
  68.0 3.2 %collective-permute-start.1 = (bf16[3,448,512]{2,1,0:T(8,128)(2,1)S(1)}, bf16[3,448,512]{2,1,0:T(8,128)(2,1)}, u32[]{:S(2)}, u32[]{:S(2)}) collective-permute-start(bf16[3,448,512]{2,1,0:T(8,128)(2,1)S(1)} %pad_maximum_fusion.mine), channel_id=1, source_target_pairs={{0,1},{1,0},{2,3},{3,2},{4,5},{5,4},{6,7},{7,6},{8,9},{9,8},{10,11... | collective-permute-start | bytes 4128776 | tf_op jit(solution)/shard_map/ppermute | solution.py:38
  71.1 1.9 %collective-permute-start.2 = (bf16[3,448,512]{2,1,0:T(8,128)(2,1)S(1)}, bf16[3,448,512]{2,1,0:T(8,128)(2,1)}, u32[]{:S(2)}, u32[]{:S(2)}) collective-permute-start(bf16[3,448,512]{2,1,0:T(8,128)(2,1)S(1)} %collective-permute-done.beside), channel_id=1, source_target_pairs={{0,1},{1,0},{2,3},{3,2},{4,5},{5,4},{6,7},{7,6},{8,9},{9,8},{10,11... | collective-permute-start | bytes 4128776 | tf_op jit(solution)/shard_map/ppermute | solution.py:38
  73.1 8.8 %all-to-all-done.1 = bf16[8,64,512]{2,1,0:T(8,128)(2,1)S(1)} async-done(((bf16[8,64,512]{2,1,0:T(8,128)(2,1)}), bf16[8,64,512]{2,1,0:T(8,128)(2,1)S(1)}, u32[]{:S(2)}, u32[]{:S(2)}) %all-to-all-start.1) | async-done | bytes 524320 | tf_op jit(solution)/shard_map/all_to_all | solution.py:28
  81.9 0.0 collective-permute-done.1.mine_other
  81.9 0.0 collective-permute-done.2.beside_other
  81.9 3.1 %shard_map.55 = (bf16[256,1792]{1,0:T(8,128)(2,1)S(1)}, bf16[4,448,512]{2,1,0:T(8,128)(2,1)S(1)}) custom-call(bf16[2,4,64,512]{3,2,1,0:T(8,128)(2,1)S(1)} %bitcast.18, bf16[3,448,512]{2,1,0:T(8,128)(2,1)S(1)} %pad_maximum_fusion.mine, bf16[3,448,512]{2,1,0:T(8,128)(2,1)S(1)} %collective-permute-done.beside, ...), custom_call_target="tpu_custom_call" | custom-call | tf_op jit(solution)/shard_map/pallas_call | solution.py:60
  85.0 15.9 %all_to_all.31.sums_ref = bf16[8,32,1792]{2,1,0:T(8,128)(2,1)S(1)} all-to-all(bf16[8,32,1792]{2,1,0:T(8,128)(2,1)S(1)} %bitcast.20), channel_id=1, replica_groups=mesh['xl'=2,'xp'=2,'y'=4,'zh'=8,'zl'=4,'c'=2] {'xp','y'}, dimensions={0} | all-to-all | bytes 1835008 | tf_op jit(solution)/shard_map/all_to_all | solution.py:24
  100.9 0.1 shard_map.56
  101.0 11.1 %all_to_all.32.hidden_ref = bf16[8,2,32,448]{3,2,1,0:T(8,128)(2,1)S(1)} all-to-all(bf16[8,2,32,448]{3,2,1,0:T(8,128)(2,1)S(1)} %shard_map.56), channel_id=1, replica_groups=mesh['xl'=2,'xp'=2,'y'=4,'zh'=8,'zl'=4,'c'=2] {'xp','y'}, dimensions={0} | all-to-all | bytes 917504 | tf_op jit(solution)/shard_map/all_to_all | solution.py:24
  112.1 0.7 shard_map.57
  112.8 0.0 copy-start
  112.8 21.1 %all_to_all.33.parts_ref = bf16[8,64,512]{2,1,0:T(8,128)(2,1)S(1)} all-to-all(bf16[8,64,512]{2,1,0:T(8,128)(2,1)S(1)} %bitcast.19), channel_id=1, replica_groups={{0,2,4,6,512,514,516,518},{8,10,12,14,520,522,524,526},{16,18,20,22,528..., dimensions={0} | all-to-all | bytes 1048576 | tf_op jit(solution)/shard_map/all_to_all | solution.py:28
  133.9 0.1 shard_map.58
  134.0 31.6 %all_to_all.34.parts_ref = bf16[8,16,512]{2,1,0:T(8,128)(2,1)S(1)} all-to-all(bf16[8,16,512]{2,1,0:T(8,128)(2,1)S(1)} %shard_map.58), channel_id=1, replica_groups=mesh['xl'=2,'xp'=2,'y'=4,'zh'=8,'zl'=4,'c'=2] {'zh'}, dimensions={0} | all-to-all | bytes 262144 | tf_op jit(solution)/shard_map/all_to_all | solution.py:24
  165.5 0.0 copy-done
  165.5 1.2 shard_map.59
  (2 shorter events, 0.0 us)
Async XLA Ops:
  0.0 5.5 %copy-start.1 = (bf16[16,512]{1,0:T(8,128)(2,1)S(1)}, bf16[16,512]{1,0:T(8,128)(2,1)}, u32[]{:S(2)}) copy-start(bf16[16,512]{1,0:T(8,128)(2,1)} %param.5) | copy-start | bytes 49156
  1.5 60.0 %collective-permute-start = (bf16[3,448,512]{2,1,0:T(8,128)(2,1)S(1)}, bf16[3,448,512]{2,1,0:T(8,128)(2,1)S(1)}, u32[]{:S(2)}, u32[]{:S(2)}) collective-permute-start(bf16[3,448,512]{2,1,0:T(8,128)(2,1)S(1)} %pad_maximum_fusion.mine), channel_id=1, source_target_pairs={{0,512},{512,0},{1,513},{513,1},{2,514},{514,2},{3,515},{515,3},{4... | collective-permute-start | bytes 4128776 | tf_op jit(solution)/shard_map/ppermute | solution.py:38
  62.3 19.5 %all-to-all-start.1 = ((bf16[8,64,512]{2,1,0:T(8,128)(2,1)}), bf16[8,64,512]{2,1,0:T(8,128)(2,1)S(1)}, u32[]{:S(2)}, u32[]{:S(2)}) async-start(bf16[8,64,512]{2,1,0:T(8,128)(2,1)} %bitcast.21), calls=%async_computation.1 | async-start | bytes 1048576 | tf_op jit(solution)/shard_map/all_to_all | solution.py:28
  68.0 13.9 %collective-permute-start.1 = (bf16[3,448,512]{2,1,0:T(8,128)(2,1)S(1)}, bf16[3,448,512]{2,1,0:T(8,128)(2,1)}, u32[]{:S(2)}, u32[]{:S(2)}) collective-permute-start(bf16[3,448,512]{2,1,0:T(8,128)(2,1)S(1)} %pad_maximum_fusion.mine), channel_id=1, source_target_pairs={{0,1},{1,0},{2,3},{3,2},{4,5},{5,4},{6,7},{7,6},{8,9},{9,8},{10,11... | collective-permute-start | bytes 4128776 | tf_op jit(solution)/shard_map/ppermute | solution.py:38
  71.1 10.7 %collective-permute-start.2 = (bf16[3,448,512]{2,1,0:T(8,128)(2,1)S(1)}, bf16[3,448,512]{2,1,0:T(8,128)(2,1)}, u32[]{:S(2)}, u32[]{:S(2)}) collective-permute-start(bf16[3,448,512]{2,1,0:T(8,128)(2,1)S(1)} %collective-permute-done.beside), channel_id=1, source_target_pairs={{0,1},{1,0},{2,3},{3,2},{4,5},{5,4},{6,7},{7,6},{8,9},{9,8},{10,11... | collective-permute-start | bytes 4128776 | tf_op jit(solution)/shard_map/ppermute | solution.py:38
  112.8 52.7 %copy-start = (s32[16]{0:T(128)S(1)}, s32[16]{0:T(128)}, u32[]{:S(2)}) copy-start(s32[16]{0:T(128)} %mask_ref) | copy-start | bytes 196
